TPU v7x, 32 devices: a whole 2x2x4 slice. The times are simulated.
32 devices in a mesh: replica: 4 (over z), fsdp: 4 (over y, core), tensor: 2 (over x).
Axes of the slice: x: 2, y: 2, z: 4, core: 2. Of those that a mesh axis runs over, the one named last changes fastest.
Arguments:
- tokens: bfloat16 [2, 1536, 5120], P(None, ('replica', 'fsdp')), may hold values from -6 to 6
- cotangent: bfloat16 [2, 1536, 7168], P(None, 'replica', ('fsdp', 'tensor')), may hold values from -6 to 6
- gate_weight: bfloat16 [4, 5120, 7168], P('replica', None, ('fsdp', 'tensor')), may hold values from -6 to 6
- up_weight: bfloat16 [4, 5120, 7168], P('replica', None, ('fsdp', 'tensor')), may hold values from -6 to 6
Outputs:
- gate_final: bfloat16 [4, 5120, 7168], P('replica', None, ('fsdp', 'tensor'))
- up_final: bfloat16 [4, 5120, 7168], P('replica', None, ('fsdp', 'tensor'))
All inputs are finite; a program needn't handle non-finite values.
Results may differ from a plain program's by a relative error of at most 0.0052.
Values may be sent and summed in bfloat16 or wider, within the bound.
A program may use at most 256 MiB of HBM per device.

v0:
```python
import jax
import jax.numpy as jnp
from jax import lax
from jax.sharding import PartitionSpec as P

learn_rate = 1.0


def from_partner(value, axis, bit):
    mask = 2**bit
    pairs = [(source, source ^ mask) for source in range(lax.axis_size(axis))]
    return lax.ppermute(value, axis, pairs)


def per_device(tokens, cotangent, gate_weight, up_weight):
    gate_w = gate_weight[0]
    up_w = up_weight[0]
    factor = float(tokens.shape[2]) ** (-0.5)
    for section in range(cotangent.shape[0]):
        inputs = lax.all_gather(tokens[section], "fsdp", axis=0, tiled=True)
        partner_gate, partner_up = from_partner((gate_w, up_w), "replica", section)
        gate_pre = jnp.dot(inputs, gate_w, preferred_element_type=jnp.float32) * factor
        up_pre = jnp.dot(inputs, up_w, preferred_element_type=jnp.float32) * factor
        logistic = jax.nn.sigmoid(gate_pre)
        grad_in = cotangent[section].astype(jnp.float32)
        d_up = (grad_in * gate_pre * logistic).astype(jnp.bfloat16)
        d_gate = (grad_in * up_pre * logistic * (1.0 + gate_pre * (1.0 - logistic))).astype(
            jnp.bfloat16
        )
        grad_gate = jnp.dot(inputs.T, d_gate, preferred_element_type=jnp.float32) * factor
        grad_up = jnp.dot(inputs.T, d_up, preferred_element_type=jnp.float32) * factor
        own_gate = gate_w.astype(jnp.float32) - learn_rate * grad_gate
        own_up = up_w.astype(jnp.float32) - learn_rate * grad_up
        gate_w = (0.5 * own_gate + 0.5 * partner_gate.astype(jnp.float32)).astype(jnp.bfloat16)
        up_w = (0.5 * own_up + 0.5 * partner_up.astype(jnp.float32)).astype(jnp.bfloat16)
    return (gate_w[None], up_w[None])


def solution(mesh):
    return jax.shard_map(
        per_device,
        mesh=mesh,
        in_specs=(
            P(None, ("replica", "fsdp"), None),
            P(None, "replica", ("fsdp", "tensor")),
            P("replica", None, ("fsdp", "tensor")),
            P("replica", None, ("fsdp", "tensor")),
        ),
        out_specs=(P("replica", None, ("fsdp", "tensor")), P("replica", None, ("fsdp", "tensor"))),
        check_vma=False,
    )
```

profile of v0, /device:TPU:0, one launch (start us, length us, event | category | flops | bytes accessed | tf_op | source)
XLA Modules:
  0.0 1073.6 jit_solution(6739525559883604689)
XLA Ops:
  7.2 0.0 copy-start.1
  7.2 0.0 all-gather.5.cloned.1.call-start
  7.2 12.9 %copy.6 = bf16[1,5120,896]{1,2,0:T(8,128)(2,1)} copy(bf16[1,5120,896]{2,1,0:T(8,128)(2,1)} %param.6) | data formatting | bytes 18350080 | tf_op args[2]
  20.1 3.0 collective-permute-start
  23.1 0.0 copy-done.1
  23.1 1.4 fusion.103
  24.5 0.0 all-gather.5.cloned.1.call-update
  24.5 0.0 all-gather.7.cloned.1.call-start
  24.6 13.1 %copy.7 = bf16[1,5120,896]{1,2,0:T(8,128)(2,1)} copy(bf16[1,5120,896]{2,1,0:T(8,128)(2,1)} %param.7) | data formatting | bytes 18350080 | tf_op args[3]
  37.7 0.0 collective-permute-start.1
  37.7 0.0 all-gather.7.cloned.1.call-update
  37.7 0.0 copy-start.2
  37.7 20.2 %all-gather.5.cloned.1.call-done = bf16[1,384,5120]{2,1,0:T(8,128)(2,1)} async-done(((bf16[1,96,5120]{2,1,0:T(8,128)(2,1)}), bf16[1,384,5120]{2,1,0:T(8,128)(2,1)}) %all-gather.5.cloned.1.call-update) | async-done | bytes 3932176 | tf_op jit(solution)/shard_map/all_gather | solution.py:20
  57.9 9.6 fusion.35
  67.6 154.0 %collective-permute-done = bf16[5120,896]{0,1:T(8,128)(2,1)} collective-permute-done((bf16[5120,896]{0,1:T(8,128)(2,1)}, bf16[5120,896]{0,1:T(8,128)(2,1)}, u32[]{:S(2)}, u32[]{:S(2)}) %collective-permute-start) | collective-permute-done | bytes 9175072 | tf_op jit(solution)/shard_map/ppermute | solution.py:12
  221.6 0.0 copy-done.2
  221.6 26.9 %fusion.11 = bf16[5120,896]{0,1:T(8,128)(2,1)} fusion(bf16[5120,896]{0,1:T(8,128)(2,1)} %collective-permute-done, bf16[1,384,5120]{2,1,0:T(8,128)(2,1)} %all-gather.5.cloned.1.call-done, f32[384,896]{1,0:T(8,128)S(1)} %fusion.35, bf16[1,5120,896]{2,1,0:T(8,128)(2,1)} %param.7, bf16[2,384,896]{2,1,0:T(8,128)(2,1)S(1)} %copy-done.2, ...), kind=kOutput, calls=%fused_computation.15 | convolution fusion | flops 7082672128 | bytes 46628864 | tf_op jit(solution)/shard_map/dot_general | solution.py:30
  248.5 3.1 collective-permute-start.2
  251.5 334.7 %collective-permute-done.1 = bf16[5120,896]{0,1:T(8,128)(2,1)} collective-permute-done((bf16[5120,896]{0,1:T(8,128)(2,1)}, bf16[5120,896]{0,1:T(8,128)(2,1)}, u32[]{:S(2)}, u32[]{:S(2)}) %collective-permute-start.1) | collective-permute-done | bytes 9175072 | tf_op jit(solution)/shard_map/ppermute | solution.py:12
  586.2 13.9 %fusion.8 = bf16[5120,896]{0,1:T(8,128)(2,1)} fusion(bf16[5120,896]{0,1:T(8,128)(2,1)} %collective-permute-done.1, bf16[1,384,5120]{2,1,0:T(8,128)(2,1)} %all-gather.5.cloned.1.call-done, f32[384,896]{1,0:T(8,128)S(1)} %fusion.35, bf16[2,384,896]{2,1,0:T(8,128)(2,1)S(1)} %copy-done.2, bf16[1,5120,896]{1,2,0:T(8,128)(2,1)} %copy.7), kind=kOutput, calls=%fused_computation.11 | convolution fusion | flops 3557736448 | bytes 33521664 | tf_op jit(solution)/shard_map/dot_general | solution.py:31
  600.2 0.0 collective-permute-start.3
  600.2 0.0 all-gather.7.cloned.1.call-done
  600.2 0.0 copy-start
  600.2 9.9 fusion.60
  610.1 0.0 copy-done
  610.1 9.0 fusion.18
  619.0 21.3 %fusion.20 = f32[896,5120]{1,0:T(8,128)} fusion(bf16[1,384,5120]{2,1,0:T(8,128)(2,1)} %all-gather.7.cloned.1.call-done, f32[384,896]{1,0:T(8,128)S(1)} %fusion.60, bf16[5120,896]{0,1:T(8,128)(2,1)} %fusion.8, bf16[2,384,896]{2,1,0:T(8,128)(2,1)S(1)} %copy-done.2), kind=kOutput, calls=%fused_computation.24 | convolution fusion | flops 7050559488 | bytes 37453824 | tf_op jit(solution)/shard_map/dot_general | solution.py:30
  640.3 203.0 %collective-permute-done.2 = bf16[5120,896]{0,1:T(8,128)(2,1)} collective-permute-done((bf16[5120,896]{0,1:T(8,128)(2,1)}, bf16[5120,896]{0,1:T(8,128)(2,1)}, u32[]{:S(2)}, u32[]{:S(2)}) %collective-permute-start.2) | collective-permute-done | bytes 9175072 | tf_op jit(solution)/shard_map/ppermute | solution.py:12
  843.3 16.8 %fusion.12 = bf16[1,5120,896]{1,2,0:T(8,128)(2,1)} fusion(bf16[5120,896]{0,1:T(8,128)(2,1)} %collective-permute-done.2, f32[896,5120]{1,0:T(8,128)} %fusion.20, bf16[5120,896]{0,1:T(8,128)(2,1)} %fusion.11), kind=kLoop, calls=%fused_computation.16 | loop fusion | flops 32112640 | bytes 45875200 | tf_op jit(solution)/shard_map/broadcast_in_dim | solution.py:36
  860.1 12.7 %copy.9 = bf16[1,5120,896]{2,1,0:T(8,128)(2,1)} copy(bf16[1,5120,896]{1,2,0:T(8,128)(2,1)} %fusion.12) | data formatting | bytes 18350080
  872.8 164.4 %collective-permute-done.3 = bf16[5120,896]{0,1:T(8,128)(2,1)} collective-permute-done((bf16[5120,896]{0,1:T(8,128)(2,1)}, bf16[5120,896]{0,1:T(8,128)(2,1)}, u32[]{:S(2)}, u32[]{:S(2)}) %collective-permute-start.3) | collective-permute-done | bytes 9175072 | tf_op jit(solution)/shard_map/ppermute | solution.py:12
  1037.3 16.9 %fusion.13 = bf16[1,5120,896]{1,2,0:T(8,128)(2,1)} fusion(bf16[5120,896]{0,1:T(8,128)(2,1)} %collective-permute-done.3, f32[896,5120]{1,0:T(8,128)} %fusion.18, bf16[5120,896]{0,1:T(8,128)(2,1)} %fusion.8), kind=kLoop, calls=%fused_computation.17 | loop fusion | flops 32112640 | bytes 45875200 | tf_op jit(solution)/shard_map/broadcast_in_dim | solution.py:36
  1054.1 12.7 %copy.10 = bf16[1,5120,896]{2,1,0:T(8,128)(2,1)} copy(bf16[1,5120,896]{1,2,0:T(8,128)(2,1)} %fusion.13) | data formatting | bytes 18350080
Async XLA Ops:
  7.2 16.0 %copy-start.1 = (bf16[2,96,5120]{2,1,0:T(8,128)(2,1)S(1)}, bf16[2,96,5120]{2,1,0:T(8,128)(2,1)}, u32[]{:S(2)}) copy-start(bf16[2,96,5120]{2,1,0:T(8,128)(2,1)} %param.4) | copy-start | bytes 5898244
  7.2 50.8 %all-gather.5.cloned.1.call-start = ((), (), s32[]{:S(2)}) async-start(), calls=%async_computation | async-start | bytes 4915200 | tf_op jit(solution)/shard_map/all_gather | solution.py:20
  20.1 201.5 %collective-permute-start = (bf16[5120,896]{0,1:T(8,128)(2,1)}, bf16[5120,896]{0,1:T(8,128)(2,1)}, u32[]{:S(2)}, u32[]{:S(2)}) collective-permute-start(bf16[5120,896]{0,1:T(8,128)(2,1)} %bitcast.144), channel_id=1, source_target_pairs={{0,8},{8,0},{16,24},{24,16},{1,9},{9,1},{17,25},{25,17},{2,10},{10... | collective-permute-start | bytes 27525128 | tf_op jit(solution)/shard_map/ppermute | solution.py:12
  24.5 575.6 %all-gather.7.cloned.1.call-start = ((), (), s32[]{:S(2)}) async-start(), calls=%async_computation.1 | async-start | bytes 4915200 | tf_op jit(solution)/shard_map/all_gather | solution.py:20
  37.7 548.6 %collective-permute-start.1 = (bf16[5120,896]{0,1:T(8,128)(2,1)}, bf16[5120,896]{0,1:T(8,128)(2,1)}, u32[]{:S(2)}, u32[]{:S(2)}) collective-permute-start(bf16[5120,896]{0,1:T(8,128)(2,1)} %bitcast.145), channel_id=1, source_target_pairs={{0,8},{8,0},{16,24},{24,16},{1,9},{9,1},{17,25},{25,17},{2,10},{10... | collective-permute-start | bytes 27525128 | tf_op jit(solution)/shard_map/ppermute | solution.py:12
  37.7 183.9 %copy-start.2 = (bf16[2,384,896]{2,1,0:T(8,128)(2,1)S(1)}, bf16[2,384,896]{2,1,0:T(8,128)(2,1)}, u32[]{:S(2)}) copy-start(bf16[2,384,896]{2,1,0:T(8,128)(2,1)} %param.5) | copy-start | bytes 4128772
  248.5 594.8 %collective-permute-start.2 = (bf16[5120,896]{0,1:T(8,128)(2,1)}, bf16[5120,896]{0,1:T(8,128)(2,1)}, u32[]{:S(2)}, u32[]{:S(2)}) collective-permute-start(bf16[5120,896]{0,1:T(8,128)(2,1)} %fusion.11), channel_id=1, source_target_pairs={{0,16},{8,24},{16,0},{24,8},{1,17},{9,25},{17,1},{25,9},{2,18},{10... | collective-permute-start | bytes 27525128 | tf_op jit(solution)/shard_map/ppermute | solution.py:12
  600.2 437.1 %collective-permute-start.3 = (bf16[5120,896]{0,1:T(8,128)(2,1)}, bf16[5120,896]{0,1:T(8,128)(2,1)}, u32[]{:S(2)}, u32[]{:S(2)}) collective-permute-start(bf16[5120,896]{0,1:T(8,128)(2,1)} %fusion.8), channel_id=1, source_target_pairs={{0,16},{8,24},{16,0},{24,8},{1,17},{9,25},{17,1},{25,9},{2,18},{10... | collective-permute-start | bytes 27525128 | tf_op jit(solution)/shard_map/ppermute | solution.py:12
  600.2 9.9 copy-start
Sparse Core Ops, SparseCore 0:
  24.7 33.2 all-gather.4
  59.5 32.9 all-gather.6
where the time goes:
time: 1070 us
  waiting for transfers between devices  876 us (82%)
  matrix products  90.6 us (8%)
  local copies, waits for them, and re-layouts  52.7 us (5%)
  other arithmetic  33.7 us (3%)
  between operations  14.1 us (1%)
    ppermute x4, waiting for transfers between devices, from_partner(): return lax.ppermute(value, axis, pairs)  856 us
    unnamed x10, local copies, waits for them, and re-layouts  51.3 us
    dot_general x2, matrix products, per_device(): jnp.dot(inputs.T, d_gate, preferred_element_type=jnp.float32) * factor  48.2 us
    broadcast_in_dim x2, other arithmetic, per_device(): return (gate_w[None], up_w[None])  33.7 us
    dot_general x2, matrix products, per_device(): jnp.dot(inputs.T, d_up, preferred_element_type=jnp.float32) * factor  22.9 us
  transfers between devices with their start and end apart: 6, of which 5 were waited for; matrix products, arithmetic and copies ran while one was open for 13% of the time, Pallas kernels for 0%

commit v1 on v0

v1 whole, which is shorter than its diff:
```python
import jax
import jax.numpy as jnp
from jax import lax
from jax.sharding import PartitionSpec as P

learn_rate = 1.0
GROUP = 4
CHUNKS = 20


def swap(value, mask):
    pairs = [(source, source ^ mask) for source in range(lax.axis_size("replica"))]
    return lax.ppermute(value, "replica", pairs)


def shift(value, by):
    pairs = [
        (source, source + by)
        for source in range(lax.axis_size("replica"))
        if 0 <= source % GROUP + by < GROUP
    ]
    return lax.ppermute(value, "replica", pairs)


def f32_dot(a, b):
    return jnp.dot(a, b, preferred_element_type=jnp.float32)


def backward(gate_pre, up_pre, upstream):
    logistic = jax.nn.sigmoid(gate_pre)
    grad_in = upstream.astype(jnp.float32)
    d_up = (grad_in * gate_pre * logistic).astype(jnp.bfloat16)
    d_gate = (grad_in * up_pre * logistic * (1.0 + gate_pre * (1.0 - logistic))).astype(
        jnp.bfloat16
    )
    return d_gate, d_up


def per_device(tokens, cotangent, gate_weight, up_weight):
    weights = (gate_weight[0], up_weight[0])
    depth, width = weights[0].shape
    factor = float(depth) ** (-0.5)
    place = lax.axis_index("replica") % GROUP
    rows = depth // CHUNKS

    moved = jnp.stack([swap(tokens[0], 2), swap(tokens[1], 1)])
    own = lax.all_gather(tokens, "fsdp", axis=1, tiled=True)
    moved = lax.all_gather(moved, "fsdp", axis=1, tiled=True)
    x0, x1 = own[0], own[1]
    x0_far, x1_near = moved[0], moved[1]

    near = [swap(f32_dot(x1_near, w).astype(jnp.bfloat16), 1) for w in weights]
    d0 = backward(*[f32_dot(x0, w) * factor for w in weights], cotangent[0])
    d0_far = [swap(d, 2) for d in d0]
    cross = f32_dot(x1, x0.T)
    cross_hi = cross.astype(jnp.bfloat16)
    cross_lo = (cross - cross_hi.astype(jnp.float32)).astype(jnp.bfloat16)
    pre1 = []
    for w, n, d in zip(weights, near, d0):
        drift = (f32_dot(cross_hi, d) + f32_dot(cross_lo, d)) * (learn_rate * factor)
        pre1.append((0.5 * factor) * (f32_dot(x1, w) + n.astype(jnp.float32) - drift))
    d1 = backward(*pre1, cotangent[1])
    lefts = jnp.concatenate([x0, x0_far, x1], axis=0)
    rights = [
        jnp.concatenate([a, b, 2.0 * c], axis=0) for a, b, c in zip(d0, d0_far, d1)
    ]

    def piece(w, index):
        index = jnp.clip(index, 0, CHUNKS - 1)
        return lax.dynamic_slice_in_dim(w, index * rows, rows, axis=0)

    arrived = {(m, by): [] for m in range(2) for by in (1, -1)}
    for step in range(CHUNKS + GROUP - 2):
        for m in range(2):
            for by in (1, -1):
                rank = place if by == 1 else GROUP - 1 - place
                block = piece(weights[m], step - rank)
                if step:
                    before = arrived[m, by][-1].astype(jnp.float32)
                    block = (before + block.astype(jnp.float32)).astype(jnp.bfloat16)
                arrived[m, by].append(shift(block, by))

    outs = []
    for m in range(2):
        parts = []
        for chunk in range(CHUNKS):
            total = weights[m][chunk * rows : (chunk + 1) * rows].astype(jnp.float32)
            for by in (1, -1):
                rank = place if by == 1 else GROUP - 1 - place
                zero = jnp.zeros((rows, width), jnp.bfloat16)
                total = total + lax.select_n(
                    rank, zero, *[arrived[m, by][chunk + i] for i in range(GROUP - 1)]
                ).astype(jnp.float32)
            x = lefts[:, chunk * rows : (chunk + 1) * rows]
            grad = f32_dot(x.T, rights[m])
            parts.append((0.25 * total - (0.25 * learn_rate * factor) * grad).astype(jnp.bfloat16))
        outs.append(jnp.concatenate(parts, axis=0)[None])
    return tuple(outs)


def solution(mesh):
    return jax.shard_map(
        per_device,
        mesh=mesh,
        in_specs=(
            P(None, ("replica", "fsdp"), None),
            P(None, "replica", ("fsdp", "tensor")),
            P("replica", None, ("fsdp", "tensor")),
            P("replica", None, ("fsdp", "tensor")),
        ),
        out_specs=(P("replica", None, ("fsdp", "tensor")), P("replica", None, ("fsdp", "tensor"))),
        check_vma=False,
    )
```

time: 1070 us -> 727 us (0.68); the launches traced: 1070 us -> 714 us
  waiting for transfers between devices: 876 us -> 114 us
  starting transfers between devices: 6.18 us -> 291 us
  matrix products: 90.6 us -> 170 us
  other arithmetic: 33.7 us -> 112 us
  local copies, waits for them, and re-layouts: 52.7 us -> 10.2 us
    ppermute x4 -> x94, waiting for transfers between devices: 856 us -> 114 us  [the longest x88 91.4 us: shift(): return lax.ppermute(value, 'replica', pairs)]
    ppermute x4 -> x94, starting transfers between devices: 6.1 us -> 291 us  [the longest x88 278 us: shift(): return lax.ppermute(value, 'replica', pairs)]
    convert_element_type x0 -> x44, other arithmetic: none -> 106 us  [per_device(): block = (before + block.astype(jnp.float32)).astype(jnp.bfloat16)]
    dot_general x6 -> x51, matrix products: 90.6 us -> 170 us  [f32_dot(): return jnp.dot(a, b, preferred_element_type=jnp.float32)]
    unnamed x10 -> x304, local copies, waits for them, and re-layouts: 51.3 us -> 2.85 us
    broadcast_in_dim x2 -> x0, other arithmetic: 33.7 us -> none  [per_device(): return (gate_w[None], up_w[None])]
    all_gather x2, waiting for transfers between devices: 20.2 us -> 0.02 us  [the longest x1 0.02 us: per_device(): own = lax.all_gather(tokens, 'fsdp', axis=1, tiled=True)]
  transfers between devices with their start and end apart: 6 -> 96, of which waited for: 5 -> 43; matrix products, arithmetic and copies ran while one was open for 13% -> 40% of each run, Pallas kernels for 0% -> 0%
where the time goes in v1:
time: 727 us; the launch traced here: 714 us
  starting transfers between devices  291 us (40%)
  matrix products  170 us (23%)
  waiting for transfers between devices  114 us (16%)
  other arithmetic  112 us (15%)
  between operations  16.4 us (2%)
  local copies, waits for them, and re-layouts  10.2 us (1%)
    ppermute x88, starting transfers between devices, shift(): return lax.ppermute(value, 'replica', pairs)  278 us
    dot_general x51, matrix products, f32_dot(): return jnp.dot(a, b, preferred_element_type=jnp.float32)  170 us
    convert_element_type x44, other arithmetic, per_device(): block = (before + block.astype(jnp.float32)).astype(jnp.bfloat16)  106 us
    ppermute x88, waiting for transfers between devices, shift(): return lax.ppermute(value, 'replica', pairs)  91.4 us
    ppermute x6, waiting for transfers between devices, swap(): return lax.ppermute(value, 'replica', pairs)  22.5 us
  transfers between devices with their start and end apart: 96, of which 43 were waited for; matrix products, arithmetic and copies ran while one was open for 40% of the time, Pallas kernels for 0%

profile of v1, /device:TPU:0, one launch (start us, length us, event | category | flops | bytes accessed | tf_op | source)
XLA Modules:
  0.0 713.9 jit_solution(14769382811665063022)
XLA Ops:
  8.5 5.0 collective-permute-start
  47.8 5.7 collective-permute-start.2
  57.8 4.9 collective-permute-start.51
  67.8 5.0 collective-permute-start.11
  77.8 4.9 collective-permute-start.56
  87.9 5.7 collective-permute-start.13
  97.8 4.9 collective-permute-start.58
  107.8 5.0 collective-permute-start.15
  117.9 4.9 collective-permute-start.60
  127.8 5.7 collective-permute-start.17
  137.8 4.9 collective-permute-start.62
  147.8 5.0 collective-permute-start.19
  157.8 4.9 collective-permute-start.64
  167.8 5.7 collective-permute-start.21
  177.8 4.9 collective-permute-start.66
  187.7 5.0 collective-permute-start.23
  197.8 4.9 collective-permute-start.68
  207.8 5.7 collective-permute-start.25
  217.7 4.9 collective-permute-start.70
  227.7 5.0 collective-permute-start.27
  237.8 4.9 collective-permute-start.72
  247.7 5.7 collective-permute-start.29
  257.7 4.9 collective-permute-start.74
  267.6 5.3 collective-permute-start.31
  277.6 4.9 collective-permute-start.76
  287.7 5.7 collective-permute-start.33
  297.6 5.1 collective-permute-start.78
  307.6 5.8 collective-permute-start.35
  316.7 4.9 collective-permute-start.80
  331.8 5.8 collective-permute-start.6
  344.0 13.3 %collective-permute-done.36 = bf16[256,896]{1,0:T(8,128)(2,1)} collective-permute-done((bf16[256,896]{1,0:T(8,128)(2,1)S(1)}, bf16[256,896]{1,0:T(8,128)(2,1)}, u32[]{:S(2)}, u32[]{:S(2)}) %collective-permute-start.36) | collective-permute-done | bytes 458784 | tf_op jit(solution)/shard_map/ppermute | solution.py:22
  359.4 26.0 %collective-permute-done.37 = bf16[256,896]{1,0:T(8,128)(2,1)} collective-permute-done((bf16[256,896]{1,0:T(8,128)(2,1)}, bf16[256,896]{1,0:T(8,128)(2,1)}, u32[]{:S(2)}, u32[]{:S(2)}) %collective-permute-start.37) | collective-permute-done | bytes 458784 | tf_op jit(solution)/shard_map/ppermute | solution.py:22
  399.8 8.3 %collective-permute-start.84 = (bf16[256,896]{1,0:T(8,128)(2,1)}, bf16[256,896]{1,0:T(8,128)(2,1)}, u32[]{:S(2)}, u32[]{:S(2)}) collective-permute-start(bf16[256,896]{1,0:T(8,128)(2,1)} %get-tuple-element.10), channel_id=1, source_target_pairs={{0,8},{8,16},{16,24},{1,9},{9,17},{17,25},{2,10},{10,18},{18,26},{... | collective-permute-start | bytes 1376264 | tf_op jit(solution)/shard_map/ppermute | solution.py:22
  421.3 6.2 collective-permute-start.86
  431.7 5.0 collective-permute-start.43
  441.6 5.3 collective-permute-start.88
  451.7 5.1 collective-permute-start.45
  461.5 5.4 collective-permute-start.90
  470.9 5.1 collective-permute-done.89
  481.2 5.7 collective-permute-start.47
  495.6 9.4 %fusion.29 = (bf16[384,896]{1,0:T(8,128)(2,1)S(1)}, f32[384,896]{1,0:T(8,128)S(1)}) fusion(bf16[2,384,896]{2,1,0:T(8,128)(2,1)} %param.5, bf16[1,5120,896]{2,1,0:T(8,128)(2,1)} %param.6, bf16[2,384,5120]{2,1,0:T(8,128)(2,1)} %all-gather.3.cloned.1.call-done), kind=kOutput, calls=%fused_computation.33 | convolution fusion | flops 3525967872 | bytes 15859712 | tf_op jit(solution)/shard_map/dot_general | solution.py:26
  505.0 9.0 %fusion.41 = bf16[384,896]{1,0:T(8,128)(2,1)} fusion(f32[384,896]{1,0:T(8,128)S(1)} %get-tuple-element.93, bf16[1,5120,896]{2,1,0:T(8,128)(2,1)} %param.7, bf16[2,384,896]{2,1,0:T(8,128)(2,1)S(1)} %copy-done.139, bf16[2,384,5120]{2,1,0:T(8,128)(2,1)S(1)} %copy-done.2), kind=kOutput, calls=%fused_computation.44 | convolution fusion | flops 3527344128 | bytes 15859712 | tf_op jit(solution)/shard_map/dot_general | solution.py:26
  521.8 5.5 fusion.2
  527.3 5.3 fusion.8
  536.1 10.0 %fusion.38 = bf16[384,896]{1,0:T(8,128)(2,1)} fusion(bf16[1,5120,896]{2,1,0:T(8,128)(2,1)} %param.6, bf16[2,384,5120]{2,1,0:T(8,128)(2,1)} %all-gather.5.cloned.1.call-done), kind=kOutput, calls=%fused_computation.43 | convolution fusion | flops 3523559424 | bytes 13795328 | tf_op jit(solution)/shard_map/dot_general | solution.py:26
  546.6 7.6 %fusion.35 = bf16[384,896]{1,0:T(8,128)(2,1)} fusion(bf16[1,5120,896]{2,1,0:T(8,128)(2,1)} %param.7, bf16[2,384,5120]{2,1,0:T(8,128)(2,1)S(1)} %copy-done.4), kind=kOutput, calls=%fused_computation.42 | convolution fusion | flops 3523559424 | bytes 13795328 | tf_op jit(solution)/shard_map/dot_general | solution.py:26
  558.7 13.5 %collective-permute-done.10 = bf16[384,896]{1,0:T(8,128)(2,1)} collective-permute-done((bf16[384,896]{1,0:T(8,128)(2,1)}, bf16[384,896]{1,0:T(8,128)(2,1)}, u32[]{:S(2)}, u32[]{:S(2)}) %collective-permute-start.10) | collective-permute-done | bytes 688160 | tf_op jit(solution)/shard_map/ppermute | solution.py:13
  573.4 9.0 %collective-permute-done.9 = bf16[384,896]{1,0:T(8,128)(2,1)} collective-permute-done((bf16[384,896]{1,0:T(8,128)(2,1)}, bf16[384,896]{1,0:T(8,128)(2,1)}, u32[]{:S(2)}, u32[]{:S(2)}) %collective-permute-start.9) | collective-permute-done | bytes 688160 | tf_op jit(solution)/shard_map/ppermute | solution.py:13
  (557 shorter events, 386.5 us)
Async XLA Ops:
  7.2 488.4 %all-gather.3.cloned.1.call-start = ((), (), s32[]{:S(2)}) async-start(), calls=%async_computation | async-start | bytes 9830400 | tf_op jit(solution)/shard_map/all_gather | solution.py:47
  13.5 27.8 %collective-permute-start.3 = (bf16[256,896]{1,0:T(8,128)(2,1)S(1)}, bf16[256,896]{1,0:T(8,128)(2,1)S(1)}, u32[]{:S(2)}, u32[]{:S(2)}) collective-permute-start(bf16[256,896]{1,0:T(8,128)(2,1)S(1)} %get-tuple-element.85), channel_id=1, source_target_pairs={{8,0},{16,8},{24,16},{9,1},{17,9},{25,17},{10,2},{18,10},{26,18},{... | collective-permute-start | bytes 1376264 | tf_op jit(solution)/shard_map/ppermute | solution.py:22
  16.1 18.1 %collective-permute-start.49 = (bf16[256,896]{1,0:T(8,128)(2,1)S(1)}, bf16[256,896]{1,0:T(8,128)(2,1)S(1)}, u32[]{:S(2)}, u32[]{:S(2)}) collective-permute-start(bf16[256,896]{1,0:T(8,128)(2,1)S(1)} %get-tuple-element.42), channel_id=1, source_target_pairs={{0,8},{8,16},{16,24},{1,9},{9,17},{17,25},{2,10},{10,18},{18,26},{... | collective-permute-start | bytes 1376264 | tf_op jit(solution)/shard_map/ppermute | solution.py:22
  26.4 17.7 %collective-permute-start.1 = (bf16[256,896]{1,0:T(8,128)(2,1)}, bf16[256,896]{1,0:T(8,128)(2,1)S(1)}, u32[]{:S(2)}, u32[]{:S(2)}) collective-permute-start(bf16[256,896]{1,0:T(8,128)(2,1)} %fusion.283), channel_id=1, source_target_pairs={{0,8},{8,16},{16,24},{1,9},{9,17},{17,25},{2,10},{10,18},{18,26},{... | collective-permute-start | bytes 1376264 | tf_op jit(solution)/shard_map/ppermute | solution.py:22
  30.8 22.7 %collective-permute-start.52 = (bf16[256,896]{1,0:T(8,128)(2,1)S(1)}, bf16[256,896]{1,0:T(8,128)(2,1)S(1)}, u32[]{:S(2)}, u32[]{:S(2)}) collective-permute-start(bf16[256,896]{1,0:T(8,128)(2,1)S(1)} %get-tuple-element.43), channel_id=1, source_target_pairs={{8,0},{16,8},{24,16},{9,1},{17,9},{25,17},{10,2},{18,10},{26,18},{... | collective-permute-start | bytes 1376264 | tf_op jit(solution)/shard_map/ppermute | solution.py:22
  36.9 17.1 %collective-permute-start.50 = (bf16[256,896]{1,0:T(8,128)(2,1)}, bf16[256,896]{1,0:T(8,128)(2,1)S(1)}, u32[]{:S(2)}, u32[]{:S(2)}) collective-permute-start(bf16[256,896]{1,0:T(8,128)(2,1)} %fusion.161), channel_id=1, source_target_pairs={{0,8},{8,16},{16,24},{1,9},{9,17},{17,25},{2,10},{10,18},{18,26},{... | collective-permute-start | bytes 1376264 | tf_op jit(solution)/shard_map/ppermute | solution.py:22
  56.5 16.4 %collective-permute-start.53 = (bf16[256,896]{1,0:T(8,128)(2,1)}, bf16[256,896]{1,0:T(8,128)(2,1)S(1)}, u32[]{:S(2)}, u32[]{:S(2)}) collective-permute-start(bf16[256,896]{1,0:T(8,128)(2,1)} %get-tuple-element.41), channel_id=1, source_target_pairs={{8,0},{16,8},{24,16},{9,1},{17,9},{25,17},{10,2},{18,10},{26,18},{... | collective-permute-start | bytes 1376264 | tf_op jit(solution)/shard_map/ppermute | solution.py:22
  72.8 463.2 %all-gather.5.cloned.1.call-start = ((), (), s32[]{:S(2)}) async-start(), calls=%async_computation.1 | async-start | bytes 9830400 | tf_op jit(solution)/shard_map/all_gather | solution.py:48
  76.5 17.1 %collective-permute-start.54 = (bf16[256,896]{1,0:T(8,128)(2,1)}, bf16[256,896]{1,0:T(8,128)(2,1)S(1)}, u32[]{:S(2)}, u32[]{:S(2)}) collective-permute-start(bf16[256,896]{1,0:T(8,128)(2,1)} %get-tuple-element.39), channel_id=1, source_target_pairs={{8,0},{16,8},{24,16},{9,1},{17,9},{25,17},{10,2},{18,10},{26,18},{... | collective-permute-start | bytes 1376264 | tf_op jit(solution)/shard_map/ppermute | solution.py:22
  96.5 16.3 %collective-permute-start.57 = (bf16[256,896]{1,0:T(8,128)(2,1)}, bf16[256,896]{1,0:T(8,128)(2,1)S(1)}, u32[]{:S(2)}, u32[]{:S(2)}) collective-permute-start(bf16[256,896]{1,0:T(8,128)(2,1)} %get-tuple-element.37), channel_id=1, source_target_pairs={{8,0},{16,8},{24,16},{9,1},{17,9},{25,17},{10,2},{18,10},{26,18},{... | collective-permute-start | bytes 1376264 | tf_op jit(solution)/shard_map/ppermute | solution.py:22
  106.5 16.3 %collective-permute-start.14 = (bf16[256,896]{1,0:T(8,128)(2,1)}, bf16[256,896]{1,0:T(8,128)(2,1)S(1)}, u32[]{:S(2)}, u32[]{:S(2)}) collective-permute-start(bf16[256,896]{1,0:T(8,128)(2,1)} %get-tuple-element.77), channel_id=1, source_target_pairs={{8,0},{16,8},{24,16},{9,1},{17,9},{25,17},{10,2},{18,10},{26,18},{... | collective-permute-start | bytes 1376264 | tf_op jit(solution)/shard_map/ppermute | solution.py:22
  116.6 17.0 %collective-permute-start.59 = (bf16[256,896]{1,0:T(8,128)(2,1)}, bf16[256,896]{1,0:T(8,128)(2,1)S(1)}, u32[]{:S(2)}, u32[]{:S(2)}) collective-permute-start(bf16[256,896]{1,0:T(8,128)(2,1)} %get-tuple-element.35), channel_id=1, source_target_pairs={{8,0},{16,8},{24,16},{9,1},{17,9},{25,17},{10,2},{18,10},{26,18},{... | collective-permute-start | bytes 1376264 | tf_op jit(solution)/shard_map/ppermute | solution.py:22
  146.5 16.3 %collective-permute-start.18 = (bf16[256,896]{1,0:T(8,128)(2,1)}, bf16[256,896]{1,0:T(8,128)(2,1)S(1)}, u32[]{:S(2)}, u32[]{:S(2)}) collective-permute-start(bf16[256,896]{1,0:T(8,128)(2,1)} %get-tuple-element.73), channel_id=1, source_target_pairs={{8,0},{16,8},{24,16},{9,1},{17,9},{25,17},{10,2},{18,10},{26,18},{... | collective-permute-start | bytes 1376264 | tf_op jit(solution)/shard_map/ppermute | solution.py:22
  156.6 16.9 %collective-permute-start.63 = (bf16[256,896]{1,0:T(8,128)(2,1)}, bf16[256,896]{1,0:T(8,128)(2,1)S(1)}, u32[]{:S(2)}, u32[]{:S(2)}) collective-permute-start(bf16[256,896]{1,0:T(8,128)(2,1)} %get-tuple-element.31), channel_id=1, source_target_pairs={{8,0},{16,8},{24,16},{9,1},{17,9},{25,17},{10,2},{18,10},{26,18},{... | collective-permute-start | bytes 1376264 | tf_op jit(solution)/shard_map/ppermute | solution.py:22
  186.4 16.3 %collective-permute-start.22 = (bf16[256,896]{1,0:T(8,128)(2,1)}, bf16[256,896]{1,0:T(8,128)(2,1)S(1)}, u32[]{:S(2)}, u32[]{:S(2)}) collective-permute-start(bf16[256,896]{1,0:T(8,128)(2,1)} %get-tuple-element.69), channel_id=1, source_target_pairs={{8,0},{16,8},{24,16},{9,1},{17,9},{25,17},{10,2},{18,10},{26,18},{... | collective-permute-start | bytes 1376264 | tf_op jit(solution)/shard_map/ppermute | solution.py:22
  196.5 17.0 %collective-permute-start.67 = (bf16[256,896]{1,0:T(8,128)(2,1)}, bf16[256,896]{1,0:T(8,128)(2,1)S(1)}, u32[]{:S(2)}, u32[]{:S(2)}) collective-permute-start(bf16[256,896]{1,0:T(8,128)(2,1)} %get-tuple-element.27), channel_id=1, source_target_pairs={{8,0},{16,8},{24,16},{9,1},{17,9},{25,17},{10,2},{18,10},{26,18},{... | collective-permute-start | bytes 1376264 | tf_op jit(solution)/shard_map/ppermute | solution.py:22
  226.4 16.3 %collective-permute-start.26 = (bf16[256,896]{1,0:T(8,128)(2,1)}, bf16[256,896]{1,0:T(8,128)(2,1)S(1)}, u32[]{:S(2)}, u32[]{:S(2)}) collective-permute-start(bf16[256,896]{1,0:T(8,128)(2,1)} %get-tuple-element.65), channel_id=1, source_target_pairs={{8,0},{16,8},{24,16},{9,1},{17,9},{25,17},{10,2},{18,10},{26,18},{... | collective-permute-start | bytes 1376264 | tf_op jit(solution)/shard_map/ppermute | solution.py:22
  236.5 16.9 %collective-permute-start.71 = (bf16[256,896]{1,0:T(8,128)(2,1)}, bf16[256,896]{1,0:T(8,128)(2,1)S(1)}, u32[]{:S(2)}, u32[]{:S(2)}) collective-permute-start(bf16[256,896]{1,0:T(8,128)(2,1)} %get-tuple-element.23), channel_id=1, source_target_pairs={{8,0},{16,8},{24,16},{9,1},{17,9},{25,17},{10,2},{18,10},{26,18},{... | collective-permute-start | bytes 1376264 | tf_op jit(solution)/shard_map/ppermute | solution.py:22
  256.4 16.5 %collective-permute-start.73 = (bf16[256,896]{1,0:T(8,128)(2,1)}, bf16[256,896]{1,0:T(8,128)(2,1)S(1)}, u32[]{:S(2)}, u32[]{:S(2)}) collective-permute-start(bf16[256,896]{1,0:T(8,128)(2,1)} %get-tuple-element.21), channel_id=1, source_target_pairs={{8,0},{16,8},{24,16},{9,1},{17,9},{25,17},{10,2},{18,10},{26,18},{... | collective-permute-start | bytes 1376264 | tf_op jit(solution)/shard_map/ppermute | solution.py:22
  267.6 16.3 %collective-permute-start.31 = (bf16[256,896]{1,0:T(8,128)(2,1)}, bf16[256,896]{1,0:T(8,128)(2,1)S(1)}, u32[]{:S(2)}, u32[]{:S(2)}) collective-permute-start(bf16[256,896]{1,0:T(8,128)(2,1)} %get-tuple-element.60), channel_id=1, source_target_pairs={{0,8},{8,16},{16,24},{1,9},{9,17},{17,25},{2,10},{10,18},{18,26},{... | collective-permute-start | bytes 1376264 | tf_op jit(solution)/shard_map/ppermute | solution.py:22
  276.3 17.0 %collective-permute-start.75 = (bf16[256,896]{1,0:T(8,128)(2,1)}, bf16[256,896]{1,0:T(8,128)(2,1)S(1)}, u32[]{:S(2)}, u32[]{:S(2)}) collective-permute-start(bf16[256,896]{1,0:T(8,128)(2,1)} %get-tuple-element.19), channel_id=1, source_target_pairs={{8,0},{16,8},{24,16},{9,1},{17,9},{25,17},{10,2},{18,10},{26,18},{... | collective-permute-start | bytes 1376264 | tf_op jit(solution)/shard_map/ppermute | solution.py:22
  296.2 17.2 %collective-permute-start.77 = (bf16[256,896]{1,0:T(8,128)(2,1)}, bf16[256,896]{1,0:T(8,128)(2,1)S(1)}, u32[]{:S(2)}, u32[]{:S(2)}) collective-permute-start(bf16[256,896]{1,0:T(8,128)(2,1)} %get-tuple-element.17), channel_id=1, source_target_pairs={{8,0},{16,8},{24,16},{9,1},{17,9},{25,17},{10,2},{18,10},{26,18},{... | collective-permute-start | bytes 1376264 | tf_op jit(solution)/shard_map/ppermute | solution.py:22
  297.6 16.3 %collective-permute-start.78 = (bf16[256,896]{1,0:T(8,128)(2,1)}, bf16[256,896]{1,0:T(8,128)(2,1)S(1)}, u32[]{:S(2)}, u32[]{:S(2)}) collective-permute-start(bf16[256,896]{1,0:T(8,128)(2,1)} %get-tuple-element.16), channel_id=1, source_target_pairs={{0,8},{8,16},{16,24},{1,9},{9,17},{17,25},{2,10},{10,18},{18,26},{... | collective-permute-start | bytes 1376264 | tf_op jit(solution)/shard_map/ppermute | solution.py:22
  315.4 22.2 %collective-permute-start.79 = (bf16[256,896]{1,0:T(8,128)(2,1)S(1)}, bf16[256,896]{1,0:T(8,128)(2,1)S(1)}, u32[]{:S(2)}, u32[]{:S(2)}) collective-permute-start(bf16[256,896]{1,0:T(8,128)(2,1)S(1)} %get-tuple-element.15), channel_id=1, source_target_pairs={{8,0},{16,8},{24,16},{9,1},{17,9},{25,17},{10,2},{18,10},{26,18},{... | collective-permute-start | bytes 1376264 | tf_op jit(solution)/shard_map/ppermute | solution.py:22
  316.7 23.6 %collective-permute-start.80 = (bf16[256,896]{1,0:T(8,128)(2,1)S(1)}, bf16[256,896]{1,0:T(8,128)(2,1)S(1)}, u32[]{:S(2)}, u32[]{:S(2)}) collective-permute-start(bf16[256,896]{1,0:T(8,128)(2,1)S(1)} %get-tuple-element.14), channel_id=1, source_target_pairs={{0,8},{8,16},{16,24},{1,9},{9,17},{17,25},{2,10},{10,18},{18,26},{... | collective-permute-start | bytes 1376264 | tf_op jit(solution)/shard_map/ppermute | solution.py:22
  326.3 31.0 %collective-permute-start.36 = (bf16[256,896]{1,0:T(8,128)(2,1)S(1)}, bf16[256,896]{1,0:T(8,128)(2,1)}, u32[]{:S(2)}, u32[]{:S(2)}) collective-permute-start(bf16[256,896]{1,0:T(8,128)(2,1)S(1)} %get-tuple-element.55), channel_id=1, source_target_pairs={{8,0},{16,8},{24,16},{9,1},{17,9},{25,17},{10,2},{18,10},{26,18},{... | collective-permute-start | bytes 1376264 | tf_op jit(solution)/shard_map/ppermute | solution.py:22
  328.7 71.1 %collective-permute-start.7 = (bf16[96,5120]{1,0:T(8,128)(2,1)}, bf16[96,5120]{1,0:T(8,128)(2,1)S(1)}, u32[]{:S(2)}, u32[]{:S(2)}) collective-permute-start(bf16[96,5120]{1,0:T(8,128)(2,1)} %get-tuple-element.91), channel_id=1, source_target_pairs={{0,8},{8,0},{16,24},{24,16},{1,9},{9,1},{17,25},{25,17},{2,10},{10... | collective-permute-start | bytes 2949128 | tf_op jit(solution)/shard_map/ppermute | solution.py:13
  331.8 76.3 %collective-permute-start.6 = (bf16[96,5120]{1,0:T(8,128)(2,1)S(1)}, bf16[96,5120]{1,0:T(8,128)(2,1)S(1)}, u32[]{:S(2)}, u32[]{:S(2)}) collective-permute-start(bf16[96,5120]{1,0:T(8,128)(2,1)S(1)} %get-tuple-element.90), channel_id=1, source_target_pairs={{0,16},{8,24},{16,0},{24,8},{1,17},{9,25},{17,1},{25,9},{2,18},{10... | collective-permute-start | bytes 2949128 | tf_op jit(solution)/shard_map/ppermute | solution.py:13
  337.6 47.8 %collective-permute-start.37 = (bf16[256,896]{1,0:T(8,128)(2,1)}, bf16[256,896]{1,0:T(8,128)(2,1)}, u32[]{:S(2)}, u32[]{:S(2)}) collective-permute-start(bf16[256,896]{1,0:T(8,128)(2,1)} %get-tuple-element.54), channel_id=1, source_target_pairs={{0,8},{8,16},{16,24},{1,9},{9,17},{17,25},{2,10},{10,18},{18,26},{... | collective-permute-start | bytes 1376264 | tf_op jit(solution)/shard_map/ppermute | solution.py:22
  342.8 51.0 %collective-permute-start.81 = (bf16[256,896]{1,0:T(8,128)(2,1)}, bf16[256,896]{1,0:T(8,128)(2,1)S(1)}, u32[]{:S(2)}, u32[]{:S(2)}) collective-permute-start(bf16[256,896]{1,0:T(8,128)(2,1)} %get-tuple-element.13), channel_id=1, source_target_pairs={{8,0},{16,8},{24,16},{9,1},{17,9},{25,17},{10,2},{18,10},{26,18},{... | collective-permute-start | bytes 1376264 | tf_op jit(solution)/shard_map/ppermute | solution.py:22
  357.3 38.7 %collective-permute-start.82 = (bf16[256,896]{1,0:T(8,128)(2,1)}, bf16[256,896]{1,0:T(8,128)(2,1)}, u32[]{:S(2)}, u32[]{:S(2)}) collective-permute-start(bf16[256,896]{1,0:T(8,128)(2,1)} %get-tuple-element.12), channel_id=1, source_target_pairs={{0,8},{8,16},{16,24},{1,9},{9,17},{17,25},{2,10},{10,18},{18,26},{... | collective-permute-start | bytes 1376264 | tf_op jit(solution)/shard_map/ppermute | solution.py:22
  388.0 21.6 %collective-permute-start.38 = (bf16[256,896]{1,0:T(8,128)(2,1)}, bf16[256,896]{1,0:T(8,128)(2,1)}, u32[]{:S(2)}, u32[]{:S(2)}) collective-permute-start(bf16[256,896]{1,0:T(8,128)(2,1)} %get-tuple-element.53), channel_id=1, source_target_pairs={{8,0},{16,8},{24,16},{9,1},{17,9},{25,17},{10,2},{18,10},{26,18},{... | collective-permute-start | bytes 1376264 | tf_op jit(solution)/shard_map/ppermute | solution.py:22
  398.5 18.7 %collective-permute-start.83 = (bf16[256,896]{1,0:T(8,128)(2,1)}, bf16[256,896]{1,0:T(8,128)(2,1)}, u32[]{:S(2)}, u32[]{:S(2)}) collective-permute-start(bf16[256,896]{1,0:T(8,128)(2,1)} %get-tuple-element.11), channel_id=1, source_target_pairs={{8,0},{16,8},{24,16},{9,1},{17,9},{25,17},{10,2},{18,10},{26,18},{... | collective-permute-start | bytes 1376264 | tf_op jit(solution)/shard_map/ppermute | solution.py:22
  399.8 17.4 %collective-permute-start.84 = (bf16[256,896]{1,0:T(8,128)(2,1)}, bf16[256,896]{1,0:T(8,128)(2,1)}, u32[]{:S(2)}, u32[]{:S(2)}) collective-permute-start(bf16[256,896]{1,0:T(8,128)(2,1)} %get-tuple-element.10), channel_id=1, source_target_pairs={{0,8},{8,16},{16,24},{1,9},{9,17},{17,25},{2,10},{10,18},{18,26},{... | collective-permute-start | bytes 1376264 | tf_op jit(solution)/shard_map/ppermute | solution.py:22
  420.0 16.8 %collective-permute-start.85 = (bf16[256,896]{1,0:T(8,128)(2,1)}, bf16[256,896]{1,0:T(8,128)(2,1)S(1)}, u32[]{:S(2)}, u32[]{:S(2)}) collective-permute-start(bf16[256,896]{1,0:T(8,128)(2,1)} %get-tuple-element.9), channel_id=1, source_target_pairs={{8,0},{16,8},{24,16},{9,1},{17,9},{25,17},{10,2},{18,10},{26,18},{... | collective-permute-start | bytes 1376264 | tf_op jit(solution)/shard_map/ppermute | solution.py:22
  421.3 16.5 %collective-permute-start.86 = (bf16[256,896]{1,0:T(8,128)(2,1)S(1)}, bf16[256,896]{1,0:T(8,128)(2,1)S(1)}, u32[]{:S(2)}, u32[]{:S(2)}) collective-permute-start(bf16[256,896]{1,0:T(8,128)(2,1)S(1)} %get-tuple-element.8), channel_id=1, source_target_pairs={{0,8},{8,16},{16,24},{1,9},{9,17},{17,25},{2,10},{10,18},{18,26},{... | collective-permute-start | bytes 1376264 | tf_op jit(solution)/shard_map/ppermute | solution.py:22
  430.4 16.5 %collective-permute-start.42 = (bf16[256,896]{1,0:T(8,128)(2,1)}, bf16[256,896]{1,0:T(8,128)(2,1)S(1)}, u32[]{:S(2)}, u32[]{:S(2)}) collective-permute-start(bf16[256,896]{1,0:T(8,128)(2,1)} %get-tuple-element.49), channel_id=1, source_target_pairs={{8,0},{16,8},{24,16},{9,1},{17,9},{25,17},{10,2},{18,10},{26,18},{... | collective-permute-start | bytes 1376264 | tf_op jit(solution)/shard_map/ppermute | solution.py:22
  440.3 16.5 %collective-permute-start.87 = (bf16[256,896]{1,0:T(8,128)(2,1)}, bf16[256,896]{1,0:T(8,128)(2,1)S(1)}, u32[]{:S(2)}, u32[]{:S(2)}) collective-permute-start(bf16[256,896]{1,0:T(8,128)(2,1)} %get-tuple-element.7), channel_id=1, source_target_pairs={{8,0},{16,8},{24,16},{9,1},{17,9},{25,17},{10,2},{18,10},{26,18},{... | collective-permute-start | bytes 1376264 | tf_op jit(solution)/shard_map/ppermute | solution.py:22
  450.4 16.6 %collective-permute-start.44 = (bf16[256,896]{1,0:T(8,128)(2,1)}, bf16[256,896]{1,0:T(8,128)(2,1)S(1)}, u32[]{:S(2)}, u32[]{:S(2)}) collective-permute-start(bf16[256,896]{1,0:T(8,128)(2,1)} %get-tuple-element.47), channel_id=1, source_target_pairs={{8,0},{16,8},{24,16},{9,1},{17,9},{25,17},{10,2},{18,10},{26,18},{... | collective-permute-start | bytes 1376264 | tf_op jit(solution)/shard_map/ppermute | solution.py:22
  469.6 21.8 %collective-permute-start.46 = (bf16[256,896]{1,0:T(8,128)(2,1)}, bf16[256,896]{1,0:T(8,128)(2,1)}, u32[]{:S(2)}, u32[]{:S(2)}) collective-permute-start(bf16[256,896]{1,0:T(8,128)(2,1)} %get-tuple-element.45), channel_id=1, source_target_pairs={{8,0},{16,8},{24,16},{9,1},{17,9},{25,17},{10,2},{18,10},{26,18},{... | collective-permute-start | bytes 1376264 | tf_op jit(solution)/shard_map/ppermute | solution.py:22
  481.2 218.8 %collective-permute-start.47 = (bf16[256,896]{1,0:T(8,128)(2,1)}, bf16[256,896]{1,0:T(8,128)(2,1)}, u32[]{:S(2)}, u32[]{:S(2)}) collective-permute-start(bf16[256,896]{1,0:T(8,128)(2,1)} %get-tuple-element.44), channel_id=1, source_target_pairs={{0,8},{8,16},{16,24},{1,9},{9,17},{17,25},{2,10},{10,18},{18,26},{... | collective-permute-start | bytes 1376264 | tf_op jit(solution)/shard_map/ppermute | solution.py:22
  486.9 216.7 %collective-permute-start.92 = (bf16[256,896]{1,0:T(8,128)(2,1)}, bf16[256,896]{1,0:T(8,128)(2,1)}, u32[]{:S(2)}, u32[]{:S(2)}) collective-permute-start(bf16[256,896]{1,0:T(8,128)(2,1)} %get-tuple-element.2), channel_id=1, source_target_pairs={{0,8},{8,16},{16,24},{1,9},{9,17},{17,25},{2,10},{10,18},{18,26},{... | collective-permute-start | bytes 1376264 | tf_op jit(solution)/shard_map/ppermute | solution.py:22
  514.0 73.4 %collective-permute-start.8 = (bf16[384,896]{1,0:T(8,128)(2,1)}, bf16[384,896]{1,0:T(8,128)(2,1)}, u32[]{:S(2)}, u32[]{:S(2)}) collective-permute-start(bf16[384,896]{1,0:T(8,128)(2,1)} %fusion.41), channel_id=1, source_target_pairs={{0,16},{8,24},{16,0},{24,8},{1,17},{9,25},{17,1},{25,9},{2,18},{10... | collective-permute-start | bytes 2064392 | tf_op jit(solution)/shard_map/ppermute | solution.py:13
  546.1 26.1 %collective-permute-start.10 = (bf16[384,896]{1,0:T(8,128)(2,1)}, bf16[384,896]{1,0:T(8,128)(2,1)}, u32[]{:S(2)}, u32[]{:S(2)}) collective-permute-start(bf16[384,896]{1,0:T(8,128)(2,1)} %fusion.38), channel_id=1, source_target_pairs={{0,8},{8,0},{16,24},{24,16},{1,9},{9,1},{17,25},{25,17},{2,10},{10... | collective-permute-start | bytes 2064392 | tf_op jit(solution)/shard_map/ppermute | solution.py:13
  554.2 28.3 %collective-permute-start.9 = (bf16[384,896]{1,0:T(8,128)(2,1)}, bf16[384,896]{1,0:T(8,128)(2,1)}, u32[]{:S(2)}, u32[]{:S(2)}) collective-permute-start(bf16[384,896]{1,0:T(8,128)(2,1)} %fusion.35), channel_id=1, source_target_pairs={{0,8},{8,0},{16,24},{24,16},{1,9},{9,1},{17,25},{25,17},{2,10},{10... | collective-permute-start | bytes 2064392 | tf_op jit(solution)/shard_map/ppermute | solution.py:13
  572.1 127.9 %collective-permute-start.48 = (bf16[256,896]{1,0:T(8,128)(2,1)}, bf16[256,896]{1,0:T(8,128)(2,1)}, u32[]{:S(2)}, u32[]{:S(2)}) collective-permute-start(bf16[256,896]{1,0:T(8,128)(2,1)} %fusion.166), channel_id=1, source_target_pairs={{8,0},{16,8},{24,16},{9,1},{17,9},{25,17},{10,2},{18,10},{26,18},{... | collective-permute-start | bytes 1376264 | tf_op jit(solution)/shard_map/ppermute | solution.py:22
  582.5 121.1 %collective-permute-start.93 = (bf16[256,896]{1,0:T(8,128)(2,1)}, bf16[256,896]{1,0:T(8,128)(2,1)}, u32[]{:S(2)}, u32[]{:S(2)}) collective-permute-start(bf16[256,896]{1,0:T(8,128)(2,1)} %fusion.44), channel_id=1, source_target_pairs={{8,0},{16,8},{24,16},{9,1},{17,9},{25,17},{10,2},{18,10},{26,18},{... | collective-permute-start | bytes 1376264 | tf_op jit(solution)/shard_map/ppermute | solution.py:22
  587.5 69.8 %collective-permute-start.55 = (bf16[384,896]{1,0:T(8,128)(2,1)S(1)}, bf16[384,896]{1,0:T(8,128)(2,1)S(1)}, u32[]{:S(2)}, u32[]{:S(2)}) collective-permute-start(bf16[384,896]{1,0:T(8,128)(2,1)S(1)} %get-tuple-element.92), channel_id=1, source_target_pairs={{0,16},{8,24},{16,0},{24,8},{1,17},{9,25},{17,1},{25,9},{2,18},{10... | collective-permute-start | bytes 2064392 | tf_op jit(solution)/shard_map/ppermute | solution.py:13
  (200 other events, 2642.2 us)
Sparse Core Ops, SparseCore 0:
  73.0 56.0 all-gather.2
  409.8 54.4 all-gather.4

commit v2 on v1

v2 whole, which is shorter than its diff:
```python
import jax
import jax.numpy as jnp
from jax import lax
from jax.sharding import PartitionSpec as P

learn_rate = 1.0
GROUP = 4
CHUNKS = 20
FIRST_STEP = 4


def swap(value, mask):
    pairs = [(source, source ^ mask) for source in range(lax.axis_size("replica"))]
    return lax.ppermute(value, "replica", pairs)


def shift(value, by, step):
    pairs = []
    for source in range(lax.axis_size("replica")):
        place = source % GROUP
        rank = place if by == 1 else GROUP - 1 - place
        if 0 <= place + by < GROUP and 0 <= step - rank < CHUNKS:
            pairs.append((source, source + by))
    return lax.ppermute(value, "replica", pairs)


def gather_moved(value, mask):
    share = value.shape[0] // lax.axis_size("tensor")
    part = lax.dynamic_slice_in_dim(value, lax.axis_index("tensor") * share, share, axis=0)
    return lax.all_gather(swap(part, mask), ("fsdp", "tensor"), axis=0, tiled=True)


def f32_dot(a, b):
    return jnp.dot(a, b, preferred_element_type=jnp.float32)


def backward(gate_pre, up_pre, upstream):
    logistic = jax.nn.sigmoid(gate_pre)
    grad_in = upstream.astype(jnp.float32)
    d_up = (grad_in * gate_pre * logistic).astype(jnp.bfloat16)
    d_gate = (grad_in * up_pre * logistic * (1.0 + gate_pre * (1.0 - logistic))).astype(
        jnp.bfloat16
    )
    return d_gate, d_up


def per_device(tokens, cotangent, gate_weight, up_weight):
    weights = (gate_weight[0], up_weight[0])
    depth, width = weights[0].shape
    factor = float(depth) ** (-0.5)
    place = lax.axis_index("replica") % GROUP
    rows = depth // CHUNKS

    x1_near = gather_moved(tokens[1], 1)
    x0 = lax.all_gather(tokens[0], "fsdp", axis=0, tiled=True)
    x0_far = gather_moved(tokens[0], 2)
    x1 = lax.all_gather(tokens[1], "fsdp", axis=0, tiled=True)

    def piece(w, index):
        index = jnp.clip(index, 0, CHUNKS - 1)
        return lax.dynamic_slice_in_dim(w, index * rows, rows, axis=0)

    arrived = {(m, by): [] for m in range(2) for by in (1, -1)}
    ranks = {1: place, -1: GROUP - 1 - place}
    zero = jnp.zeros((rows, width), jnp.bfloat16)

    def final(out, m, chunk):
        start = chunk * rows
        total = weights[m][start : start + rows].astype(jnp.float32)
        for by in (1, -1):
            total = total + lax.select_n(
                ranks[by], zero, *[arrived[m, by][chunk + i] for i in range(GROUP - 1)]
            ).astype(jnp.float32)
        grad = f32_dot(lefts[:, start : start + rows].T, rights[m])
        value = 0.25 * total - (0.25 * learn_rate * factor) * grad
        return lax.dynamic_update_slice_in_dim(out, value.astype(jnp.bfloat16), start, axis=0)

    outs = [jnp.zeros((depth, width), jnp.bfloat16) for _ in range(2)]
    done = 0
    near, products = [], []
    for step in range(CHUNKS + GROUP - 2):
        ready = done
        if step > FIRST_STEP + 4:
            ready = max(done, min(done + 2, step - GROUP + 1, CHUNKS))
        for m in range(2):
            blocks = []
            for by in (1, -1):
                block = piece(weights[m], step - ranks[by])
                if step:
                    before = arrived[m, by][-1].astype(jnp.float32)
                    block = (before + block.astype(jnp.float32)).astype(jnp.bfloat16)
                blocks.append(block)
            at = (step - FIRST_STEP, m)
            if at == (0, 0):
                gate_pre0 = f32_dot(x0, weights[0]) * factor
                blocks, gate_pre0 = lax.optimization_barrier((blocks, gate_pre0))
            if at == (0, 1):
                d0 = backward(gate_pre0, f32_dot(x0, weights[1]) * factor, cotangent[0])
                blocks, d0 = lax.optimization_barrier((blocks, d0))
                d0_far = [swap(d, 2) for d in d0]
            if at[0] == 1:
                part = f32_dot(x1_near, weights[m]).astype(jnp.bfloat16)
                blocks, part = lax.optimization_barrier((blocks, part))
                near.append(swap(part, 1))
            if at == (2, 0):
                cross = f32_dot(x1, x0.T)
                cross_hi = cross.astype(jnp.bfloat16)
                cross_lo = (cross - cross_hi.astype(jnp.float32)).astype(jnp.bfloat16)
                blocks, cross_hi, cross_lo = lax.optimization_barrier(
                    (blocks, cross_hi, cross_lo)
                )
            if at[0] == 3:
                product = f32_dot(x1, weights[m])
                blocks, product = lax.optimization_barrier((blocks, product))
                products.append(product)
            if at == (4, 0):
                pre1 = []
                for product, n, d in zip(products, near, d0):
                    drift = f32_dot(cross_hi, d) + f32_dot(cross_lo, d)
                    pre1.append(
                        (0.5 * factor)
                        * (product + n.astype(jnp.float32) - (learn_rate * factor) * drift)
                    )
                d1 = backward(*pre1, cotangent[1])
                blocks, d1 = lax.optimization_barrier((blocks, d1))
            if at == (4, 1):
                lefts = jnp.concatenate([x0, x0_far, x1], axis=0)
                rights = [
                    jnp.concatenate([a, b, 2.0 * c], axis=0)
                    for a, b, c in zip(d0, d0_far, d1)
                ]
                blocks, lefts, rights = lax.optimization_barrier((blocks, lefts, rights))
            if ready > done:
                for chunk in range(done, ready):
                    outs[m] = final(outs[m], m, chunk)
                blocks, outs[m] = lax.optimization_barrier((blocks, outs[m]))
            for by, block in zip((1, -1), blocks):
                arrived[m, by].append(shift(block, by, step))
        done = ready
    for m in range(2):
        for chunk in range(done, CHUNKS):
            outs[m] = final(outs[m], m, chunk)
    return tuple(out[None] for out in outs)


def solution(mesh):
    return jax.shard_map(
        per_device,
        mesh=mesh,
        in_specs=(
            P(None, ("replica", "fsdp"), None),
            P(None, "replica", ("fsdp", "tensor")),
            P("replica", None, ("fsdp", "tensor")),
            P("replica", None, ("fsdp", "tensor")),
        ),
        out_specs=(P("replica", None, ("fsdp", "tensor")), P("replica", None, ("fsdp", "tensor"))),
        check_vma=False,
    )
```

time: 727 us -> 709 us (0.975)
  waiting for transfers between devices: 114 us -> 86.7 us
  other arithmetic: 112 us -> 93.1 us
  local copies, waits for them, and re-layouts: 10.2 us -> 24.5 us
  starting transfers between devices: 291 us -> 302 us
    ppermute x88, waiting for transfers between devices: 91.4 us -> 53.4 us  [shift(): return lax.ppermute(value, 'replica', pairs)]
    ppermute x6, starting transfers between devices: 13.4 us -> 39.4 us  [swap(): return lax.ppermute(value, 'replica', pairs)]
    convert_element_type x44 -> x41, other arithmetic: 106 us -> 82.2 us  [per_device(): block = (before + block.astype(jnp.float32)).astype(jnp.bfloat16)]
    ppermute x88, starting transfers between devices: 278 us -> 263 us  [shift(): return lax.ppermute(value, 'replica', pairs)]
    dynamic_update_slice x0 -> x2, local copies, waits for them, and re-layouts: none -> 10.8 us  [final(): lax.dynamic_update_slice_in_dim(out, value.astype(jnp.bfloat16), start, a...]
    ppermute x6, waiting for transfers between devices: 22.5 us -> 32.5 us  [swap(): return lax.ppermute(value, 'replica', pairs)]
    concatenate x1, other arithmetic: 1.11 us -> 8.46 us  [per_device(): lefts = jnp.concatenate([x0, x0_far, x1], axis=0)]
  transfers between devices with their start and end apart: 96 -> 98, of which waited for: 43 -> 26; matrix products, arithmetic and copies ran while one was open for 40% -> 40% of each run, Pallas kernels for 0% -> 0%
where the time goes in v2:
time: 709 us; the launch traced here: 696 us
  starting transfers between devices  302 us (43%)
  matrix products  173 us (24%)
  other arithmetic  93.1 us (13%)
  waiting for transfers between devices  86.7 us (12%)
  local copies, waits for them, and re-layouts  24.5 us (3%)
  between operations  16.3 us (2%)
    ppermute x88, starting transfers between devices, shift(): return lax.ppermute(value, 'replica', pairs)  263 us
    dot_general x51, matrix products, f32_dot(): return jnp.dot(a, b, preferred_element_type=jnp.float32)  173 us
    convert_element_type x41, other arithmetic, per_device(): block = (before + block.astype(jnp.float32)).astype(jnp.bfloat16)  82.2 us
    ppermute x88, waiting for transfers between devices, shift(): return lax.ppermute(value, 'replica', pairs)  53.4 us
    ppermute x6, starting transfers between devices, swap(): return lax.ppermute(value, 'replica', pairs)  39.4 us
    ppermute x6, waiting for transfers between devices, swap(): return lax.ppermute(value, 'replica', pairs)  32.5 us
  transfers between devices with their start and end apart: 98, of which 26 were waited for; matrix products, arithmetic and copies ran while one was open for 40% of the time, Pallas kernels for 0%

profile of v2, /device:TPU:0, one launch (start us, length us, event | category | flops | bytes accessed | tf_op | source)
XLA Modules:
  0.0 696.1 jit_solution(10027952360797304649)
XLA Ops:
  15.1 11.2 %collective-permute-done.10 = bf16[48,5120]{1,0:T(8,128)(2,1)S(1)} collective-permute-done((bf16[48,5120]{1,0:T(8,128)(2,1)S(1)}, bf16[48,5120]{1,0:T(8,128)(2,1)S(1)}, u32[]{:S(2)}, u32[]{:S(2)}) %collective-permute-start.10) | collective-permute-done | bytes 491552 | tf_op jit(solution)/shard_map/ppermute | solution.py:14
  37.7 6.4 collective-permute-done
  56.7 5.1 collective-permute-start.18
  66.4 5.1 collective-permute-start.2
  76.2 5.2 collective-permute-start.19
  93.3 4.8 collective-permute-done.23
  100.7 12.7 %collective-permute-start.20 = (bf16[256,896]{1,0:T(8,128)(2,1)}, bf16[256,896]{1,0:T(8,128)(2,1)S(1)}, u32[]{:S(2)}, u32[]{:S(2)}) collective-permute-start(bf16[256,896]{1,0:T(8,128)(2,1)} %get-tuple-element.287), channel_id=1, source_target_pairs={{0,8},{8,16},{16,24},{1,9},{9,17},{17,25},{2,10},{10,18},{18,26},{... | collective-permute-start | bytes 1376264 | tf_op jit(solution)/shard_map/ppermute | solution.py:24
  127.0 10.9 %fusion.12 = f32[384,896]{1,0:T(8,128)S(1)} fusion(bf16[1,5120,896]{2,1,0:T(8,128)(2,1)} %param.6, bf16[1,384,5120]{2,1,0:T(8,128)(2,1)} %all-gather.11.cloned.1.call-done), kind=kOutput, calls=%fused_computation.19 | convolution fusion | flops 3523559424 | bytes 14483456 | tf_op jit(solution)/shard_map/dot_general | solution.py:34
  138.0 9.0 %fusion.41 = bf16[384,896]{1,0:T(8,128)(2,1)} fusion(f32[384,896]{1,0:T(8,128)S(1)} %fusion.12, bf16[1,5120,896]{2,1,0:T(8,128)(2,1)} %param.7, bf16[2,384,896]{2,1,0:T(8,128)(2,1)S(1)} %copy-done.65, bf16[1,384,5120]{2,1,0:T(8,128)(2,1)S(1)} %copy-done.4), kind=kOutput, calls=%fused_computation.39 | convolution fusion | flops 3527344128 | bytes 15859712 | tf_op jit(solution)/shard_map/dot_general | solution.py:34
  147.5 11.0 %collective-permute-start.8 = (bf16[256,896]{1,0:T(8,128)(2,1)S(1)}, bf16[256,896]{1,0:T(8,128)(2,1)S(1)}, u32[]{:S(2)}, u32[]{:S(2)}) collective-permute-start(bf16[256,896]{1,0:T(8,128)(2,1)S(1)} %copy-done.22), channel_id=1, source_target_pairs={{0,8},{8,16},{16,24},{1,9},{9,17},{17,25},{2,10},{10,18},{18,26},{... | collective-permute-start | bytes 1376264 | tf_op jit(solution)/shard_map/ppermute | solution.py:24
  159.9 5.3 collective-permute-start.25
  167.0 10.2 %fusion = f32[384,896]{1,0:T(8,128)} fusion(bf16[1,5120,896]{2,1,0:T(8,128)(2,1)} %param.7, bf16[1,384,5120]{2,1,0:T(8,128)(2,1)} %all-gather.13.cloned.1.call-done), kind=kOutput, calls=%fused_computation.1 | convolution fusion | flops 3523215360 | bytes 14483456 | tf_op jit(solution)/shard_map/dot_general | solution.py:34
  177.2 8.0 %fusion.6 = f32[384,896]{1,0:T(8,128)} fusion(bf16[1,5120,896]{2,1,0:T(8,128)(2,1)} %param.6, bf16[1,384,5120]{2,1,0:T(8,128)(2,1)S(1)} %copy-done.6), kind=kOutput, calls=%fused_computation.7 | convolution fusion | flops 3523215360 | bytes 14483456 | tf_op jit(solution)/shard_map/dot_general | solution.py:34
  193.4 10.0 %fusion.35 = bf16[384,896]{1,0:T(8,128)(2,1)} fusion(bf16[384,5120]{1,0:T(8,128)(2,1)} %all-gather.7.cloned.1.call-done, bf16[1,5120,896]{2,1,0:T(8,128)(2,1)} %param.6), kind=kOutput, calls=%fused_computation.37 | convolution fusion | flops 3523559424 | bytes 13795328 | tf_op jit(solution)/shard_map/dot_general | solution.py:34
  203.4 5.3 collective-permute-start.11
  210.0 7.7 %fusion.38 = bf16[384,896]{1,0:T(8,128)(2,1)} fusion(bf16[384,5120]{1,0:T(8,128)(2,1)S(1)} %copy-done.67, bf16[1,5120,896]{2,1,0:T(8,128)(2,1)} %param.7), kind=kOutput, calls=%fused_computation.38 | convolution fusion | flops 3523559424 | bytes 13795328 | tf_op jit(solution)/shard_map/dot_general | solution.py:34
  217.7 5.3 collective-permute-start.27
  227.1 8.5 %pad_maximum_fusion = bf16[1152,5120]{1,0:T(8,128)(2,1)S(1)} fusion(bf16[384,5120]{1,0:T(8,128)(2,1)} %bitcast.517, bf16[384,5120]{1,0:T(8,128)(2,1)} %all-gather.9.cloned.1.call-done, bf16[384,5120]{1,0:T(8,128)(2,1)} %bitcast.516), kind=kLoop, calls=%fused_computation | loop fusion | flops 35389440 | bytes 23592960 | tf_op jit(solution)/shard_map/concatenate | solution.py:127
  235.6 4.9 fusion.276
  246.9 4.6 collective-permute-start.13
  258.8 4.6 collective-permute-done.30
  266.4 27.9 %collective-permute-start.31 = (bf16[384,896]{1,0:T(8,128)(2,1)S(1)}, bf16[384,896]{1,0:T(8,128)(2,1)S(1)}, u32[]{:S(2)}, u32[]{:S(2)}) collective-permute-start(bf16[384,896]{1,0:T(8,128)(2,1)S(1)} %copy-done.68), channel_id=1, source_target_pairs={{0,8},{8,0},{16,24},{24,16},{1,9},{9,1},{17,25},{25,17},{2,10},{10... | collective-permute-start | bytes 2064392 | tf_op jit(solution)/shard_map/ppermute | solution.py:14
  294.6 7.6 %collective-permute-start.15 = (bf16[256,896]{1,0:T(8,128)(2,1)S(1)}, bf16[256,896]{1,0:T(8,128)(2,1)S(1)}, u32[]{:S(2)}, u32[]{:S(2)}) collective-permute-start(bf16[256,896]{1,0:T(8,128)(2,1)S(1)} %get-tuple-element.118), channel_id=1, source_target_pairs={{0,8},{8,16},{16,24},{1,9},{9,17},{17,25},{2,10},{10,18},{18,26},{... | collective-permute-start | bytes 1376264 | tf_op jit(solution)/shard_map/ppermute | solution.py:24
  305.7 17.4 %collective-permute-done.31 = bf16[384,896]{1,0:T(8,128)(2,1)S(1)} collective-permute-done((bf16[384,896]{1,0:T(8,128)(2,1)S(1)}, bf16[384,896]{1,0:T(8,128)(2,1)S(1)}, u32[]{:S(2)}, u32[]{:S(2)}) %collective-permute-start.31) | collective-permute-done | bytes 688160 | tf_op jit(solution)/shard_map/ppermute | solution.py:14
  326.9 8.4 %collective-permute-done.16 = bf16[256,896]{1,0:T(8,128)(2,1)S(1)} collective-permute-done((bf16[256,896]{1,0:T(8,128)(2,1)S(1)}, bf16[256,896]{1,0:T(8,128)(2,1)S(1)}, u32[]{:S(2)}, u32[]{:S(2)}) %collective-permute-start.16) | collective-permute-done | bytes 458784 | tf_op jit(solution)/shard_map/ppermute | solution.py:24
  338.5 5.3 collective-permute-done.36
  345.0 7.0 %collective-permute-start.66 = (bf16[256,896]{1,0:T(8,128)(2,1)}, bf16[256,896]{1,0:T(8,128)(2,1)}, u32[]{:S(2)}, u32[]{:S(2)}) collective-permute-start(bf16[256,896]{1,0:T(8,128)(2,1)} %get-tuple-element.180), channel_id=1, source_target_pairs={{0,8},{8,16},{16,24},{1,9},{9,17},{17,25},{2,10},{10,18},{18,26},{... | collective-permute-start | bytes 1376264 | tf_op jit(solution)/shard_map/ppermute | solution.py:24
  356.5 5.3 dynamic_update_slice.144
  365.9 5.4 dynamic_update_slice.124
  371.4 6.5 collective-permute-start.33
  389.5 5.2 collective-permute-start.68
  397.2 4.7 collective-permute-start.40
  416.0 5.3 collective-permute-start.70
  425.0 5.4 collective-permute-start.42
  445.3 6.0 collective-permute-start.72
  455.0 5.5 collective-permute-start.44
  480.7 4.6 collective-permute-start.46
  498.2 4.6 collective-permute-start.76
  506.5 4.6 collective-permute-start.48
  519.6 5.0 collective-permute-start.78
  528.3 5.4 collective-permute-start.50
  541.6 5.0 collective-permute-start.80
  550.9 4.6 collective-permute-start.52
  562.7 4.6 collective-permute-start.82
  603.5 4.7 collective-permute-start.86
  611.7 5.3 collective-permute-start.58
  624.2 4.7 collective-permute-start.88
  648.5 5.6 collective-permute-done.61
  (422 shorter events, 342.4 us)
Async XLA Ops:
  7.2 119.8 %all-gather.11.cloned.1.call-start = ((), (), s32[]{:S(2)}) async-start(), calls=%async_computation.2 | async-start | bytes 4915200 | tf_op jit(solution)/shard_map/all_gather | solution.py:55
  10.1 156.9 %all-gather.13.cloned.1.call-start = ((), (), s32[]{:S(2)}) async-start(), calls=%async_computation.3 | async-start | bytes 4915200 | tf_op jit(solution)/shard_map/all_gather | solution.py:57
  10.9 182.5 %all-gather.7.cloned.1.call-start = ((), (), s32[]{:S(2)}) async-start(), calls=%async_computation | async-start | bytes 4423680 | tf_op jit(solution)/shard_map/all_gather | solution.py:30
  27.1 199.9 %all-gather.9.cloned.1.call-start = ((), (), s32[]{:S(2)}) async-start(), calls=%async_computation.1 | async-start | bytes 4423680 | tf_op jit(solution)/shard_map/all_gather | solution.py:30
  66.4 19.8 %collective-permute-start.2 = (bf16[256,896]{1,0:T(8,128)(2,1)}, bf16[256,896]{1,0:T(8,128)(2,1)}, u32[]{:S(2)}, u32[]{:S(2)}) collective-permute-start(bf16[256,896]{1,0:T(8,128)(2,1)} %get-tuple-element.307), channel_id=1, source_target_pairs={{0,8},{8,16},{16,24},{1,9},{9,17},{17,25},{2,10},{10,18},{18,26},{... | collective-permute-start | bytes 1376264 | tf_op jit(solution)/shard_map/ppermute | solution.py:24
  82.7 36.0 %collective-permute-start.37 = (bf16[48,5120]{1,0:T(8,128)(2,1)S(1)}, bf16[48,5120]{1,0:T(8,128)(2,1)S(1)}, u32[]{:S(2)}, u32[]{:S(2)}) collective-permute-start(bf16[48,5120]{1,0:T(8,128)(2,1)S(1)} %dynamic-slice_bitcast_fusion), channel_id=1, source_target_pairs={{0,16},{8,24},{16,0},{24,8},{1,17},{9,25},{17,1},{25,9},{2,18},{10... | collective-permute-start | bytes 1474568 | tf_op jit(solution)/shard_map/ppermute | solution.py:14
  88.8 30.8 %collective-permute-start.3 = (bf16[256,896]{1,0:T(8,128)(2,1)}, bf16[256,896]{1,0:T(8,128)(2,1)S(1)}, u32[]{:S(2)}, u32[]{:S(2)}) collective-permute-start(bf16[256,896]{1,0:T(8,128)(2,1)} %get-tuple-element.305), channel_id=1, source_target_pairs={{0,8},{8,16},{16,24},{1,9},{9,17},{17,25},{2,10},{10,18},{18,26},{... | collective-permute-start | bytes 1376264 | tf_op jit(solution)/shard_map/ppermute | solution.py:24
  91.5 28.0 %collective-permute-start.7 = (bf16[256,896]{1,0:T(8,128)(2,1)}, bf16[256,896]{1,0:T(8,128)(2,1)S(1)}, u32[]{:S(2)}, u32[]{:S(2)}) collective-permute-start(bf16[256,896]{1,0:T(8,128)(2,1)} %get-tuple-element.304), channel_id=1, source_target_pairs={{8,0},{16,8},{24,16},{9,1},{17,9},{25,17},{10,2},{18,10},{26,18},{... | collective-permute-start | bytes 1376264 | tf_op jit(solution)/shard_map/ppermute | solution.py:24
  100.7 20.8 %collective-permute-start.20 = (bf16[256,896]{1,0:T(8,128)(2,1)}, bf16[256,896]{1,0:T(8,128)(2,1)S(1)}, u32[]{:S(2)}, u32[]{:S(2)}) collective-permute-start(bf16[256,896]{1,0:T(8,128)(2,1)} %get-tuple-element.287), channel_id=1, source_target_pairs={{0,8},{8,16},{16,24},{1,9},{9,17},{17,25},{2,10},{10,18},{18,26},{... | collective-permute-start | bytes 1376264 | tf_op jit(solution)/shard_map/ppermute | solution.py:24
  147.5 40.6 %collective-permute-start.8 = (bf16[256,896]{1,0:T(8,128)(2,1)S(1)}, bf16[256,896]{1,0:T(8,128)(2,1)S(1)}, u32[]{:S(2)}, u32[]{:S(2)}) collective-permute-start(bf16[256,896]{1,0:T(8,128)(2,1)S(1)} %copy-done.22), channel_id=1, source_target_pairs={{0,8},{8,16},{16,24},{1,9},{9,17},{17,25},{2,10},{10,18},{18,26},{... | collective-permute-start | bytes 1376264 | tf_op jit(solution)/shard_map/ppermute | solution.py:24
  158.6 29.5 %collective-permute-start.9 = (bf16[256,896]{1,0:T(8,128)(2,1)S(1)}, bf16[256,896]{1,0:T(8,128)(2,1)}, u32[]{:S(2)}, u32[]{:S(2)}) collective-permute-start(bf16[256,896]{1,0:T(8,128)(2,1)S(1)} %copy-done.21), channel_id=1, source_target_pairs={{8,0},{16,8},{24,16},{9,1},{17,9},{25,17},{10,2},{18,10},{26,18},{... | collective-permute-start | bytes 1376264 | tf_op jit(solution)/shard_map/ppermute | solution.py:24
  159.9 30.9 %collective-permute-start.25 = (bf16[256,896]{1,0:T(8,128)(2,1)S(1)}, bf16[256,896]{1,0:T(8,128)(2,1)}, u32[]{:S(2)}, u32[]{:S(2)}) collective-permute-start(bf16[256,896]{1,0:T(8,128)(2,1)S(1)} %get-tuple-element.121), channel_id=1, source_target_pairs={{0,8},{8,16},{16,24},{1,9},{9,17},{17,25},{2,10},{10,18},{18,26},{... | collective-permute-start | bytes 1376264 | tf_op jit(solution)/shard_map/ppermute | solution.py:24
  165.2 25.6 %collective-permute-start.26 = (bf16[256,896]{1,0:T(8,128)(2,1)S(1)}, bf16[256,896]{1,0:T(8,128)(2,1)}, u32[]{:S(2)}, u32[]{:S(2)}) collective-permute-start(bf16[256,896]{1,0:T(8,128)(2,1)S(1)} %get-tuple-element.122), channel_id=1, source_target_pairs={{8,0},{16,8},{24,16},{9,1},{17,9},{25,17},{10,2},{18,10},{26,18},{... | collective-permute-start | bytes 1376264 | tf_op jit(solution)/shard_map/ppermute | solution.py:24
  203.4 32.2 %collective-permute-start.11 = (bf16[256,896]{1,0:T(8,128)(2,1)}, bf16[256,896]{1,0:T(8,128)(2,1)}, u32[]{:S(2)}, u32[]{:S(2)}) collective-permute-start(bf16[256,896]{1,0:T(8,128)(2,1)} %get-tuple-element.114), channel_id=1, source_target_pairs={{0,8},{8,16},{16,24},{1,9},{9,17},{17,25},{2,10},{10,18},{18,26},{... | collective-permute-start | bytes 1376264 | tf_op jit(solution)/shard_map/ppermute | solution.py:24
  208.7 26.9 %collective-permute-start.12 = (bf16[256,896]{1,0:T(8,128)(2,1)}, bf16[256,896]{1,0:T(8,128)(2,1)}, u32[]{:S(2)}, u32[]{:S(2)}) collective-permute-start(bf16[256,896]{1,0:T(8,128)(2,1)} %get-tuple-element.115), channel_id=1, source_target_pairs={{8,0},{16,8},{24,16},{9,1},{17,9},{25,17},{10,2},{18,10},{26,18},{... | collective-permute-start | bytes 1376264 | tf_op jit(solution)/shard_map/ppermute | solution.py:24
  217.7 22.8 %collective-permute-start.27 = (bf16[256,896]{1,0:T(8,128)(2,1)}, bf16[256,896]{1,0:T(8,128)(2,1)}, u32[]{:S(2)}, u32[]{:S(2)}) collective-permute-start(bf16[256,896]{1,0:T(8,128)(2,1)} %get-tuple-element.123), channel_id=1, source_target_pairs={{0,8},{8,16},{16,24},{1,9},{9,17},{17,25},{2,10},{10,18},{18,26},{... | collective-permute-start | bytes 1376264 | tf_op jit(solution)/shard_map/ppermute | solution.py:24
  224.3 77.9 %collective-permute-start.32 = (bf16[384,896]{1,0:T(8,128)(2,1)}, bf16[384,896]{1,0:T(8,128)(2,1)}, u32[]{:S(2)}, u32[]{:S(2)}) collective-permute-start(bf16[384,896]{1,0:T(8,128)(2,1)} %fusion.35), channel_id=1, source_target_pairs={{0,8},{8,0},{16,24},{24,16},{1,9},{9,1},{17,25},{25,17},{2,10},{10... | collective-permute-start | bytes 2064392 | tf_op jit(solution)/shard_map/ppermute | solution.py:14
  246.9 19.5 %collective-permute-start.13 = (bf16[256,896]{1,0:T(8,128)(2,1)S(1)}, bf16[256,896]{1,0:T(8,128)(2,1)S(1)}, u32[]{:S(2)}, u32[]{:S(2)}) collective-permute-start(bf16[256,896]{1,0:T(8,128)(2,1)S(1)} %get-tuple-element.116), channel_id=1, source_target_pairs={{0,8},{8,16},{16,24},{1,9},{9,17},{17,25},{2,10},{10,18},{18,26},{... | collective-permute-start | bytes 1376264 | tf_op jit(solution)/shard_map/ppermute | solution.py:24
  251.5 42.8 %collective-permute-start.14 = (bf16[256,896]{1,0:T(8,128)(2,1)S(1)}, bf16[256,896]{1,0:T(8,128)(2,1)S(1)}, u32[]{:S(2)}, u32[]{:S(2)}) collective-permute-start(bf16[256,896]{1,0:T(8,128)(2,1)S(1)} %get-tuple-element.117), channel_id=1, source_target_pairs={{8,0},{16,8},{24,16},{9,1},{17,9},{25,17},{10,2},{18,10},{26,18},{... | collective-permute-start | bytes 1376264 | tf_op jit(solution)/shard_map/ppermute | solution.py:24
  256.6 80.0 %collective-permute-start.39 = (bf16[384,896]{1,0:T(8,128)(2,1)S(1)}, bf16[384,896]{1,0:T(8,128)(2,1)S(1)}, u32[]{:S(2)}, u32[]{:S(2)}) collective-permute-start(bf16[384,896]{1,0:T(8,128)(2,1)S(1)} %fusion.29), channel_id=1, source_target_pairs={{0,16},{8,24},{16,0},{24,8},{1,17},{9,25},{17,1},{25,9},{2,18},{10... | collective-permute-start | bytes 2064392 | tf_op jit(solution)/shard_map/ppermute | solution.py:14
  263.5 73.4 %collective-permute-start.38 = (bf16[384,896]{1,0:T(8,128)(2,1)S(1)}, bf16[384,896]{1,0:T(8,128)(2,1)S(1)}, u32[]{:S(2)}, u32[]{:S(2)}) collective-permute-start(bf16[384,896]{1,0:T(8,128)(2,1)S(1)} %copy-done.7), channel_id=1, source_target_pairs={{0,16},{8,24},{16,0},{24,8},{1,17},{9,25},{17,1},{25,9},{2,18},{10... | collective-permute-start | bytes 2064392 | tf_op jit(solution)/shard_map/ppermute | solution.py:14
  266.4 56.6 %collective-permute-start.31 = (bf16[384,896]{1,0:T(8,128)(2,1)S(1)}, bf16[384,896]{1,0:T(8,128)(2,1)S(1)}, u32[]{:S(2)}, u32[]{:S(2)}) collective-permute-start(bf16[384,896]{1,0:T(8,128)(2,1)S(1)} %copy-done.68), channel_id=1, source_target_pairs={{0,8},{8,0},{16,24},{24,16},{1,9},{9,1},{17,25},{25,17},{2,10},{10... | collective-permute-start | bytes 2064392 | tf_op jit(solution)/shard_map/ppermute | solution.py:14
  294.6 30.8 %collective-permute-start.15 = (bf16[256,896]{1,0:T(8,128)(2,1)S(1)}, bf16[256,896]{1,0:T(8,128)(2,1)S(1)}, u32[]{:S(2)}, u32[]{:S(2)}) collective-permute-start(bf16[256,896]{1,0:T(8,128)(2,1)S(1)} %get-tuple-element.118), channel_id=1, source_target_pairs={{0,8},{8,16},{16,24},{1,9},{9,17},{17,25},{2,10},{10,18},{18,26},{... | collective-permute-start | bytes 1376264 | tf_op jit(solution)/shard_map/ppermute | solution.py:24
  302.2 33.1 %collective-permute-start.16 = (bf16[256,896]{1,0:T(8,128)(2,1)S(1)}, bf16[256,896]{1,0:T(8,128)(2,1)S(1)}, u32[]{:S(2)}, u32[]{:S(2)}) collective-permute-start(bf16[256,896]{1,0:T(8,128)(2,1)S(1)} %get-tuple-element.119), channel_id=1, source_target_pairs={{8,0},{16,8},{24,16},{9,1},{17,9},{25,17},{10,2},{18,10},{26,18},{... | collective-permute-start | bytes 1376264 | tf_op jit(solution)/shard_map/ppermute | solution.py:24
  345.0 42.1 %collective-permute-start.66 = (bf16[256,896]{1,0:T(8,128)(2,1)}, bf16[256,896]{1,0:T(8,128)(2,1)}, u32[]{:S(2)}, u32[]{:S(2)}) collective-permute-start(bf16[256,896]{1,0:T(8,128)(2,1)} %get-tuple-element.180), channel_id=1, source_target_pairs={{0,8},{8,16},{16,24},{1,9},{9,17},{17,25},{2,10},{10,18},{18,26},{... | collective-permute-start | bytes 1376264 | tf_op jit(solution)/shard_map/ppermute | solution.py:24
  351.9 35.1 %collective-permute-start.67 = (bf16[256,896]{1,0:T(8,128)(2,1)}, bf16[256,896]{1,0:T(8,128)(2,1)}, u32[]{:S(2)}, u32[]{:S(2)}) collective-permute-start(bf16[256,896]{1,0:T(8,128)(2,1)} %get-tuple-element.181), channel_id=1, source_target_pairs={{8,0},{16,8},{24,16},{9,1},{17,9},{25,17},{10,2},{18,10},{26,18},{... | collective-permute-start | bytes 1376264 | tf_op jit(solution)/shard_map/ppermute | solution.py:24
  371.4 24.6 %collective-permute-start.33 = (bf16[256,896]{1,0:T(8,128)(2,1)}, bf16[256,896]{1,0:T(8,128)(2,1)S(1)}, u32[]{:S(2)}, u32[]{:S(2)}) collective-permute-start(bf16[256,896]{1,0:T(8,128)(2,1)} %get-tuple-element.133), channel_id=1, source_target_pairs={{0,8},{8,16},{16,24},{1,9},{9,17},{17,25},{2,10},{10,18},{18,26},{... | collective-permute-start | bytes 1376264 | tf_op jit(solution)/shard_map/ppermute | solution.py:24
  389.5 25.3 %collective-permute-start.68 = (bf16[256,896]{1,0:T(8,128)(2,1)}, bf16[256,896]{1,0:T(8,128)(2,1)S(1)}, u32[]{:S(2)}, u32[]{:S(2)}) collective-permute-start(bf16[256,896]{1,0:T(8,128)(2,1)} %get-tuple-element.183), channel_id=1, source_target_pairs={{0,8},{8,16},{16,24},{1,9},{9,17},{17,25},{2,10},{10,18},{18,26},{... | collective-permute-start | bytes 1376264 | tf_op jit(solution)/shard_map/ppermute | solution.py:24
  394.6 20.1 %collective-permute-start.69 = (bf16[256,896]{1,0:T(8,128)(2,1)}, bf16[256,896]{1,0:T(8,128)(2,1)S(1)}, u32[]{:S(2)}, u32[]{:S(2)}) collective-permute-start(bf16[256,896]{1,0:T(8,128)(2,1)} %get-tuple-element.184), channel_id=1, source_target_pairs={{8,0},{16,8},{24,16},{9,1},{17,9},{25,17},{10,2},{18,10},{26,18},{... | collective-permute-start | bytes 1376264 | tf_op jit(solution)/shard_map/ppermute | solution.py:24
  397.2 25.4 %collective-permute-start.40 = (bf16[256,896]{1,0:T(8,128)(2,1)}, bf16[256,896]{1,0:T(8,128)(2,1)S(1)}, u32[]{:S(2)}, u32[]{:S(2)}) collective-permute-start(bf16[256,896]{1,0:T(8,128)(2,1)} %get-tuple-element.141), channel_id=1, source_target_pairs={{0,8},{8,16},{16,24},{1,9},{9,17},{17,25},{2,10},{10,18},{18,26},{... | collective-permute-start | bytes 1376264 | tf_op jit(solution)/shard_map/ppermute | solution.py:24
  401.9 20.7 %collective-permute-start.41 = (bf16[256,896]{1,0:T(8,128)(2,1)}, bf16[256,896]{1,0:T(8,128)(2,1)}, u32[]{:S(2)}, u32[]{:S(2)}) collective-permute-start(bf16[256,896]{1,0:T(8,128)(2,1)} %get-tuple-element.142), channel_id=1, source_target_pairs={{8,0},{16,8},{24,16},{9,1},{17,9},{25,17},{10,2},{18,10},{26,18},{... | collective-permute-start | bytes 1376264 | tf_op jit(solution)/shard_map/ppermute | solution.py:24
  416.0 27.0 %collective-permute-start.70 = (bf16[256,896]{1,0:T(8,128)(2,1)}, bf16[256,896]{1,0:T(8,128)(2,1)}, u32[]{:S(2)}, u32[]{:S(2)}) collective-permute-start(bf16[256,896]{1,0:T(8,128)(2,1)} %get-tuple-element.186), channel_id=1, source_target_pairs={{0,8},{8,16},{16,24},{1,9},{9,17},{17,25},{2,10},{10,18},{18,26},{... | collective-permute-start | bytes 1376264 | tf_op jit(solution)/shard_map/ppermute | solution.py:24
  421.3 21.7 %collective-permute-start.71 = (bf16[256,896]{1,0:T(8,128)(2,1)}, bf16[256,896]{1,0:T(8,128)(2,1)}, u32[]{:S(2)}, u32[]{:S(2)}) collective-permute-start(bf16[256,896]{1,0:T(8,128)(2,1)} %get-tuple-element.187), channel_id=1, source_target_pairs={{8,0},{16,8},{24,16},{9,1},{17,9},{25,17},{10,2},{18,10},{26,18},{... | collective-permute-start | bytes 1376264 | tf_op jit(solution)/shard_map/ppermute | solution.py:24
  425.0 27.7 %collective-permute-start.42 = (bf16[256,896]{1,0:T(8,128)(2,1)}, bf16[256,896]{1,0:T(8,128)(2,1)}, u32[]{:S(2)}, u32[]{:S(2)}) collective-permute-start(bf16[256,896]{1,0:T(8,128)(2,1)} %get-tuple-element.144), channel_id=1, source_target_pairs={{0,8},{8,16},{16,24},{1,9},{9,17},{17,25},{2,10},{10,18},{18,26},{... | collective-permute-start | bytes 1376264 | tf_op jit(solution)/shard_map/ppermute | solution.py:24
  430.4 22.2 %collective-permute-start.43 = (bf16[256,896]{1,0:T(8,128)(2,1)}, bf16[256,896]{1,0:T(8,128)(2,1)}, u32[]{:S(2)}, u32[]{:S(2)}) collective-permute-start(bf16[256,896]{1,0:T(8,128)(2,1)} %get-tuple-element.145), channel_id=1, source_target_pairs={{8,0},{16,8},{24,16},{9,1},{17,9},{25,17},{10,2},{18,10},{26,18},{... | collective-permute-start | bytes 1376264 | tf_op jit(solution)/shard_map/ppermute | solution.py:24
  445.3 27.0 %collective-permute-start.72 = (bf16[256,896]{1,0:T(8,128)(2,1)}, bf16[256,896]{1,0:T(8,128)(2,1)}, u32[]{:S(2)}, u32[]{:S(2)}) collective-permute-start(bf16[256,896]{1,0:T(8,128)(2,1)} %get-tuple-element.189), channel_id=1, source_target_pairs={{0,8},{8,16},{16,24},{1,9},{9,17},{17,25},{2,10},{10,18},{18,26},{... | collective-permute-start | bytes 1376264 | tf_op jit(solution)/shard_map/ppermute | solution.py:24
  451.3 21.0 %collective-permute-start.73 = (bf16[256,896]{1,0:T(8,128)(2,1)}, bf16[256,896]{1,0:T(8,128)(2,1)}, u32[]{:S(2)}, u32[]{:S(2)}) collective-permute-start(bf16[256,896]{1,0:T(8,128)(2,1)} %get-tuple-element.190), channel_id=1, source_target_pairs={{8,0},{16,8},{24,16},{9,1},{17,9},{25,17},{10,2},{18,10},{26,18},{... | collective-permute-start | bytes 1376264 | tf_op jit(solution)/shard_map/ppermute | solution.py:24
  455.0 23.4 %collective-permute-start.44 = (bf16[256,896]{1,0:T(8,128)(2,1)}, bf16[256,896]{1,0:T(8,128)(2,1)}, u32[]{:S(2)}, u32[]{:S(2)}) collective-permute-start(bf16[256,896]{1,0:T(8,128)(2,1)} %get-tuple-element.147), channel_id=1, source_target_pairs={{0,8},{8,16},{16,24},{1,9},{9,17},{17,25},{2,10},{10,18},{18,26},{... | collective-permute-start | bytes 1376264 | tf_op jit(solution)/shard_map/ppermute | solution.py:24
  474.6 23.4 %collective-permute-start.74 = (bf16[256,896]{1,0:T(8,128)(2,1)}, bf16[256,896]{1,0:T(8,128)(2,1)S(1)}, u32[]{:S(2)}, u32[]{:S(2)}) collective-permute-start(bf16[256,896]{1,0:T(8,128)(2,1)} %get-tuple-element.192), channel_id=1, source_target_pairs={{0,8},{8,16},{16,24},{1,9},{9,17},{17,25},{2,10},{10,18},{18,26},{... | collective-permute-start | bytes 1376264 | tf_op jit(solution)/shard_map/ppermute | solution.py:24
  477.0 20.9 %collective-permute-start.75 = (bf16[256,896]{1,0:T(8,128)(2,1)S(1)}, bf16[256,896]{1,0:T(8,128)(2,1)S(1)}, u32[]{:S(2)}, u32[]{:S(2)}) collective-permute-start(bf16[256,896]{1,0:T(8,128)(2,1)S(1)} %get-tuple-element.193), channel_id=1, source_target_pairs={{8,0},{16,8},{24,16},{9,1},{17,9},{25,17},{10,2},{18,10},{26,18},{... | collective-permute-start | bytes 1376264 | tf_op jit(solution)/shard_map/ppermute | solution.py:24
  480.7 23.4 %collective-permute-start.46 = (bf16[256,896]{1,0:T(8,128)(2,1)}, bf16[256,896]{1,0:T(8,128)(2,1)S(1)}, u32[]{:S(2)}, u32[]{:S(2)}) collective-permute-start(bf16[256,896]{1,0:T(8,128)(2,1)} %get-tuple-element.150), channel_id=1, source_target_pairs={{0,8},{8,16},{16,24},{1,9},{9,17},{17,25},{2,10},{10,18},{18,26},{... | collective-permute-start | bytes 1376264 | tf_op jit(solution)/shard_map/ppermute | solution.py:24
  498.2 20.2 %collective-permute-start.76 = (bf16[256,896]{1,0:T(8,128)(2,1)S(1)}, bf16[256,896]{1,0:T(8,128)(2,1)S(1)}, u32[]{:S(2)}, u32[]{:S(2)}) collective-permute-start(bf16[256,896]{1,0:T(8,128)(2,1)S(1)} %get-tuple-element.195), channel_id=1, source_target_pairs={{0,8},{8,16},{16,24},{1,9},{9,17},{17,25},{2,10},{10,18},{18,26},{... | collective-permute-start | bytes 1376264 | tf_op jit(solution)/shard_map/ppermute | solution.py:24
  506.5 19.4 %collective-permute-start.48 = (bf16[256,896]{1,0:T(8,128)(2,1)}, bf16[256,896]{1,0:T(8,128)(2,1)S(1)}, u32[]{:S(2)}, u32[]{:S(2)}) collective-permute-start(bf16[256,896]{1,0:T(8,128)(2,1)} %get-tuple-element.153), channel_id=1, source_target_pairs={{0,8},{8,16},{16,24},{1,9},{9,17},{17,25},{2,10},{10,18},{18,26},{... | collective-permute-start | bytes 1376264 | tf_op jit(solution)/shard_map/ppermute | solution.py:24
  519.6 20.8 %collective-permute-start.78 = (bf16[256,896]{1,0:T(8,128)(2,1)}, bf16[256,896]{1,0:T(8,128)(2,1)S(1)}, u32[]{:S(2)}, u32[]{:S(2)}) collective-permute-start(bf16[256,896]{1,0:T(8,128)(2,1)} %get-tuple-element.198), channel_id=1, source_target_pairs={{0,8},{8,16},{16,24},{1,9},{9,17},{17,25},{2,10},{10,18},{18,26},{... | collective-permute-start | bytes 1376264 | tf_op jit(solution)/shard_map/ppermute | solution.py:24
  528.3 19.6 %collective-permute-start.50 = (bf16[256,896]{1,0:T(8,128)(2,1)}, bf16[256,896]{1,0:T(8,128)(2,1)}, u32[]{:S(2)}, u32[]{:S(2)}) collective-permute-start(bf16[256,896]{1,0:T(8,128)(2,1)} %get-tuple-element.156), channel_id=1, source_target_pairs={{0,8},{8,16},{16,24},{1,9},{9,17},{17,25},{2,10},{10,18},{18,26},{... | collective-permute-start | bytes 1376264 | tf_op jit(solution)/shard_map/ppermute | solution.py:24
  541.6 19.9 %collective-permute-start.80 = (bf16[256,896]{1,0:T(8,128)(2,1)}, bf16[256,896]{1,0:T(8,128)(2,1)S(1)}, u32[]{:S(2)}, u32[]{:S(2)}) collective-permute-start(bf16[256,896]{1,0:T(8,128)(2,1)} %get-tuple-element.201), channel_id=1, source_target_pairs={{0,8},{8,16},{16,24},{1,9},{9,17},{17,25},{2,10},{10,18},{18,26},{... | collective-permute-start | bytes 1376264 | tf_op jit(solution)/shard_map/ppermute | solution.py:24
  562.7 19.7 %collective-permute-start.82 = (bf16[256,896]{1,0:T(8,128)(2,1)}, bf16[256,896]{1,0:T(8,128)(2,1)S(1)}, u32[]{:S(2)}, u32[]{:S(2)}) collective-permute-start(bf16[256,896]{1,0:T(8,128)(2,1)} %get-tuple-element.204), channel_id=1, source_target_pairs={{0,8},{8,16},{16,24},{1,9},{9,17},{17,25},{2,10},{10,18},{18,26},{... | collective-permute-start | bytes 1376264 | tf_op jit(solution)/shard_map/ppermute | solution.py:24
  603.5 19.4 %collective-permute-start.86 = (bf16[256,896]{1,0:T(8,128)(2,1)}, bf16[256,896]{1,0:T(8,128)(2,1)S(1)}, u32[]{:S(2)}, u32[]{:S(2)}) collective-permute-start(bf16[256,896]{1,0:T(8,128)(2,1)} %get-tuple-element.210), channel_id=1, source_target_pairs={{0,8},{8,16},{16,24},{1,9},{9,17},{17,25},{2,10},{10,18},{18,26},{... | collective-permute-start | bytes 1376264 | tf_op jit(solution)/shard_map/ppermute | solution.py:24
  (131 other events, 2857.0 us)
Sparse Core Ops, SparseCore 0:
  10.2 35.6 all-gather.10
  48.1 32.9 all-gather.12
  83.0 35.6 all-gather.6
  120.4 35.6 all-gather.8

commit v3 on v2

--- a/solution.py
+++ b/solution.py
@@ -5,8 +5,8 @@
 
 learn_rate = 1.0
 GROUP = 4
-CHUNKS = 20
-FIRST_STEP = 4
+CHUNKS = 10
+FIRST_STEP = 2
 
 
 def swap(value, mask):

time: 709 us -> 657 us (0.927)
  waiting for transfers between devices: 86.7 us -> 237 us
  starting transfers between devices: 302 us -> 154 us
  other arithmetic: 93.1 us -> 69.1 us
  matrix products: 173 us -> 152 us
    ppermute x88 -> x48, starting transfers between devices: 263 us -> 128 us  [shift(): return lax.ppermute(value, 'replica', pairs)]
    ppermute x88 -> x48, waiting for transfers between devices: 53.4 us -> 174 us  [shift(): return lax.ppermute(value, 'replica', pairs)]
    ppermute x6, waiting for transfers between devices: 32.5 us -> 62.5 us  [swap(): return lax.ppermute(value, 'replica', pairs)]
    convert_element_type x41 -> x21, other arithmetic: 82.2 us -> 59.9 us  [per_device(): block = (before + block.astype(jnp.float32)).astype(jnp.bfloat16)]
    dot_general x51 -> x31, matrix products: 173 us -> 152 us  [f32_dot(): return jnp.dot(a, b, preferred_element_type=jnp.float32)]
    ppermute x6, starting transfers between devices: 39.4 us -> 25.6 us  [swap(): return lax.ppermute(value, 'replica', pairs)]
  transfers between devices with their start and end apart: 98 -> 58, of which waited for: 26 -> 27; matrix products, arithmetic and copies ran while one was open for 40% -> 35% of each run, Pallas kernels for 0% -> 0%
where the time goes in v3:
time: 657 us; the launch traced here: 647 us
  waiting for transfers between devices  237 us (36%)
  starting transfers between devices  154 us (23%)
  matrix products  152 us (23%)
  other arithmetic  69.1 us (11%)
  local copies, waits for them, and re-layouts  19.3 us (3%)
  between operations  15.2 us (2%)
    ppermute x48, waiting for transfers between devices, shift(): return lax.ppermute(value, 'replica', pairs)  174 us
    dot_general x31, matrix products, f32_dot(): return jnp.dot(a, b, preferred_element_type=jnp.float32)  152 us
    ppermute x48, starting transfers between devices, shift(): return lax.ppermute(value, 'replica', pairs)  128 us
    ppermute x6, waiting for transfers between devices, swap(): return lax.ppermute(value, 'replica', pairs)  62.5 us
    convert_element_type x21, other arithmetic, per_device(): block = (before + block.astype(jnp.float32)).astype(jnp.bfloat16)  59.9 us
    ppermute x6, starting transfers between devices, swap(): return lax.ppermute(value, 'replica', pairs)  25.6 us
  transfers between devices with their start and end apart: 58, of which 27 were waited for; matrix products, arithmetic and copies ran while one was open for 35% of the time, Pallas kernels for 0%

profile of v3, /device:TPU:0, one launch (start us, length us, event | category | flops | bytes accessed | tf_op | source)
XLA Modules:
  0.0 647.0 jit_solution(10003167769834297189)
XLA Ops:
  14.4 11.2 %collective-permute-done.6 = bf16[48,5120]{1,0:T(8,128)(2,1)S(1)} collective-permute-done((bf16[48,5120]{1,0:T(8,128)(2,1)S(1)}, bf16[48,5120]{1,0:T(8,128)(2,1)S(1)}, u32[]{:S(2)}, u32[]{:S(2)}) %collective-permute-start.6) | collective-permute-done | bytes 491552 | tf_op jit(solution)/shard_map/ppermute | solution.py:14
  40.3 13.6 %collective-permute-done = bf16[512,896]{1,0:T(8,128)(2,1)S(1)} collective-permute-done((bf16[512,896]{1,0:T(8,128)(2,1)}, bf16[512,896]{1,0:T(8,128)(2,1)S(1)}, u32[]{:S(2)}, u32[]{:S(2)}) %collective-permute-start) | collective-permute-done | bytes 917536 | tf_op jit(solution)/shard_map/ppermute | solution.py:24
  63.1 10.5 %collective-permute-done.13 = bf16[512,896]{1,0:T(8,128)(2,1)} collective-permute-done((bf16[512,896]{1,0:T(8,128)(2,1)}, bf16[512,896]{1,0:T(8,128)(2,1)}, u32[]{:S(2)}, u32[]{:S(2)}) %collective-permute-start.13) | collective-permute-done | bytes 917536 | tf_op jit(solution)/shard_map/ppermute | solution.py:24
  77.3 5.4 collective-permute-start.14
  87.3 34.1 %collective-permute-done.29 = bf16[48,5120]{1,0:T(8,128)(2,1)S(1)} collective-permute-done((bf16[48,5120]{1,0:T(8,128)(2,1)S(1)}, bf16[48,5120]{1,0:T(8,128)(2,1)S(1)}, u32[]{:S(2)}, u32[]{:S(2)}) %collective-permute-start.29) | collective-permute-done | bytes 491552 | tf_op jit(solution)/shard_map/ppermute | solution.py:14
  122.3 5.3 fusion.120
  127.6 10.3 %fusion.136 = f32[384,896]{1,0:T(8,128)S(1)} fusion(bf16[1,5120,896]{2,1,0:T(8,128)(2,1)} %param.6, bf16[1,384,5120]{2,1,0:T(8,128)(2,1)} %all-gather.11.cloned.1.call-done), kind=kOutput, calls=%fused_computation.207 | convolution fusion | flops 3523559424 | bytes 14483456 | tf_op jit(solution)/shard_map/dot_general | solution.py:34
  138.4 8.1 %fusion.179 = bf16[384,896]{1,0:T(8,128)(2,1)S(1)} fusion(f32[384,896]{1,0:T(8,128)S(1)} %fusion.136, bf16[1,5120,896]{2,1,0:T(8,128)(2,1)} %param.7, bf16[2,384,896]{2,1,0:T(8,128)(2,1)S(1)} %copy-done.35, bf16[1,384,5120]{2,1,0:T(8,128)(2,1)S(1)} %copy-done.3), kind=kOutput, calls=%fused_computation.241 | convolution fusion | flops 3527344128 | bytes 15859712 | tf_op jit(solution)/shard_map/dot_general | solution.py:34
  146.5 7.0 %collective-permute-start.4 = (bf16[512,896]{1,0:T(8,128)(2,1)}, bf16[512,896]{1,0:T(8,128)(2,1)}, u32[]{:S(2)}, u32[]{:S(2)}) collective-permute-start(bf16[512,896]{1,0:T(8,128)(2,1)} %get-tuple-element.64), channel_id=1, source_target_pairs={{0,8},{8,16},{16,24},{1,9},{9,17},{17,25},{2,10},{10,18},{18,26},{... | collective-permute-start | bytes 2752520 | tf_op jit(solution)/shard_map/ppermute | solution.py:24
  154.8 5.6 collective-permute-start.17
  162.2 10.1 %fusion = f32[384,896]{1,0:T(8,128)} fusion(bf16[1,5120,896]{2,1,0:T(8,128)(2,1)} %param.7, bf16[1,384,5120]{2,1,0:T(8,128)(2,1)} %all-gather.13.cloned.1.call-done), kind=kOutput, calls=%fused_computation.1 | convolution fusion | flops 3523215360 | bytes 14483456 | tf_op jit(solution)/shard_map/dot_general | solution.py:34
  173.7 5.3 collective-permute-done.5
  182.7 7.6 %collective-permute-done.17 = bf16[512,896]{1,0:T(8,128)(2,1)} collective-permute-done((bf16[512,896]{1,0:T(8,128)(2,1)}, bf16[512,896]{1,0:T(8,128)(2,1)}, u32[]{:S(2)}, u32[]{:S(2)}) %collective-permute-start.17) | collective-permute-done | bytes 917536 | tf_op jit(solution)/shard_map/ppermute | solution.py:24
  190.3 5.0 collective-permute-done.18
  199.2 10.0 %fusion.173 = bf16[384,896]{1,0:T(8,128)(2,1)} fusion(bf16[384,5120]{1,0:T(8,128)(2,1)} %all-gather.7.cloned.1.call-done, bf16[1,5120,896]{2,1,0:T(8,128)(2,1)} %param.6), kind=kOutput, calls=%fused_computation.239 | convolution fusion | flops 3523559424 | bytes 13795328 | tf_op jit(solution)/shard_map/dot_general | solution.py:34
  212.7 8.4 %fusion.176 = bf16[384,896]{1,0:T(8,128)(2,1)} fusion(bf16[384,5120]{1,0:T(8,128)(2,1)S(1)} %copy-done.37, bf16[1,5120,896]{2,1,0:T(8,128)(2,1)} %param.7), kind=kOutput, calls=%fused_computation.240 | convolution fusion | flops 3523559424 | bytes 13795328 | tf_op jit(solution)/shard_map/dot_general | solution.py:34
  226.8 5.3 fusion.6
  239.5 12.0 %collective-permute-done.19 = bf16[512,896]{1,0:T(8,128)(2,1)S(1)} collective-permute-done((bf16[512,896]{1,0:T(8,128)(2,1)S(1)}, bf16[512,896]{1,0:T(8,128)(2,1)S(1)}, u32[]{:S(2)}, u32[]{:S(2)}) %collective-permute-start.19) | collective-permute-done | bytes 917536 | tf_op jit(solution)/shard_map/ppermute | solution.py:24
  264.7 6.1 collective-permute-start.9
  270.8 8.2 %pad_maximum_fusion = bf16[1152,5120]{1,0:T(8,128)(2,1)S(1)} fusion(bf16[384,5120]{1,0:T(8,128)(2,1)} %bitcast.319, bf16[384,5120]{1,0:T(8,128)(2,1)} %all-gather.9.cloned.1.call-done, bf16[384,5120]{1,0:T(8,128)(2,1)} %bitcast.318), kind=kLoop, calls=%fused_computation | loop fusion | flops 35389440 | bytes 23592960 | tf_op jit(solution)/shard_map/concatenate | solution.py:127
  280.2 5.8 collective-permute-done.20
  286.0 7.2 %collective-permute-done.22 = bf16[512,896]{1,0:T(8,128)(2,1)} collective-permute-done((bf16[512,896]{1,0:T(8,128)(2,1)}, bf16[512,896]{1,0:T(8,128)(2,1)}, u32[]{:S(2)}, u32[]{:S(2)}) %collective-permute-start.22) | collective-permute-done | bytes 917536 | tf_op jit(solution)/shard_map/ppermute | solution.py:24
  295.2 20.6 %collective-permute-done.10 = bf16[512,896]{1,0:T(8,128)(2,1)} collective-permute-done((bf16[512,896]{1,0:T(8,128)(2,1)}, bf16[512,896]{1,0:T(8,128)(2,1)}, u32[]{:S(2)}, u32[]{:S(2)}) %collective-permute-start.10) | collective-permute-done | bytes 917536 | tf_op jit(solution)/shard_map/ppermute | solution.py:24
  315.8 17.0 %collective-permute-start.23 = (bf16[384,896]{1,0:T(8,128)(2,1)S(1)}, bf16[384,896]{1,0:T(8,128)(2,1)S(1)}, u32[]{:S(2)}, u32[]{:S(2)}) collective-permute-start(bf16[384,896]{1,0:T(8,128)(2,1)S(1)} %copy-done.38), channel_id=1, source_target_pairs={{0,8},{8,0},{16,24},{24,16},{1,9},{9,1},{17,25},{25,17},{2,10},{10... | collective-permute-start | bytes 2064392 | tf_op jit(solution)/shard_map/ppermute | solution.py:14
  340.8 17.2 %collective-permute-done.23 = bf16[384,896]{1,0:T(8,128)(2,1)S(1)} collective-permute-done((bf16[384,896]{1,0:T(8,128)(2,1)S(1)}, bf16[384,896]{1,0:T(8,128)(2,1)S(1)}, u32[]{:S(2)}, u32[]{:S(2)}) %collective-permute-start.23) | collective-permute-done | bytes 688160 | tf_op jit(solution)/shard_map/ppermute | solution.py:14
  360.4 9.2 %collective-permute-done.11 = bf16[512,896]{1,0:T(8,128)(2,1)S(1)} collective-permute-done((bf16[512,896]{1,0:T(8,128)(2,1)S(1)}, bf16[512,896]{1,0:T(8,128)(2,1)S(1)}, u32[]{:S(2)}, u32[]{:S(2)}) %collective-permute-start.11) | collective-permute-done | bytes 917536 | tf_op jit(solution)/shard_map/ppermute | solution.py:24
  370.8 4.8 collective-permute-done.12
  379.6 5.5 collective-permute-done.27
  385.1 8.7 %collective-permute-done.28 = bf16[512,896]{1,0:T(8,128)(2,1)S(1)} collective-permute-done((bf16[512,896]{1,0:T(8,128)(2,1)S(1)}, bf16[512,896]{1,0:T(8,128)(2,1)S(1)}, u32[]{:S(2)}, u32[]{:S(2)}) %collective-permute-start.28) | collective-permute-done | bytes 917536 | tf_op jit(solution)/shard_map/ppermute | solution.py:24
  395.5 7.1 %collective-permute-start.42 = (bf16[512,896]{1,0:T(8,128)(2,1)}, bf16[512,896]{1,0:T(8,128)(2,1)}, u32[]{:S(2)}, u32[]{:S(2)}) collective-permute-start(bf16[512,896]{1,0:T(8,128)(2,1)} %get-tuple-element.108), channel_id=1, source_target_pairs={{0,8},{8,16},{16,24},{1,9},{9,17},{17,25},{2,10},{10,18},{18,26},{... | collective-permute-start | bytes 2752520 | tf_op jit(solution)/shard_map/ppermute | solution.py:24
  403.9 6.7 %collective-permute-start.25 = (bf16[512,896]{1,0:T(8,128)(2,1)}, bf16[512,896]{1,0:T(8,128)(2,1)}, u32[]{:S(2)}, u32[]{:S(2)}) collective-permute-start(bf16[512,896]{1,0:T(8,128)(2,1)} %get-tuple-element.85), channel_id=1, source_target_pairs={{0,8},{8,16},{16,24},{1,9},{9,17},{17,25},{2,10},{10,18},{18,26},{... | collective-permute-start | bytes 2752520 | tf_op jit(solution)/shard_map/ppermute | solution.py:24
  420.5 5.5 fusion.157
  434.6 5.5 fusion.150
  443.3 5.0 collective-permute-start.44
  453.0 4.9 collective-permute-start.32
  459.6 5.1 fusion.158
  469.4 4.9 fusion.151
  480.5 5.1 collective-permute-start.46
  489.9 5.5 collective-permute-start.34
  506.0 4.7 fusion.153
  517.3 4.9 collective-permute-start.48
  542.6 5.0 collective-permute-done.49
  552.5 14.8 %collective-permute-done.37 = bf16[512,896]{1,0:T(8,128)(2,1)S(1)} collective-permute-done((bf16[512,896]{1,0:T(8,128)(2,1)}, bf16[512,896]{1,0:T(8,128)(2,1)S(1)}, u32[]{:S(2)}, u32[]{:S(2)}) %collective-permute-start.37) | collective-permute-done | bytes 917536 | tf_op jit(solution)/shard_map/ppermute | solution.py:24
  580.0 7.1 %collective-permute-done.51 = bf16[512,896]{1,0:T(8,128)(2,1)} collective-permute-done((bf16[512,896]{1,0:T(8,128)(2,1)}, bf16[512,896]{1,0:T(8,128)(2,1)}, u32[]{:S(2)}, u32[]{:S(2)}) %collective-permute-start.51) | collective-permute-done | bytes 917536 | tf_op jit(solution)/shard_map/ppermute | solution.py:24
  591.8 14.9 %collective-permute-done.39 = bf16[512,896]{1,0:T(8,128)(2,1)} collective-permute-done((bf16[512,896]{1,0:T(8,128)(2,1)}, bf16[512,896]{1,0:T(8,128)(2,1)}, u32[]{:S(2)}, u32[]{:S(2)}) %collective-permute-start.39) | collective-permute-done | bytes 917536 | tf_op jit(solution)/shard_map/ppermute | solution.py:24
  625.4 4.7 fusion.189
  630.2 5.1 collective-permute-done.41
  635.3 4.7 fusion.185
  (249 shorter events, 225.3 us)
Async XLA Ops:
  7.2 120.4 %all-gather.11.cloned.1.call-start = ((), (), s32[]{:S(2)}) async-start(), calls=%async_computation.2 | async-start | bytes 4915200 | tf_op jit(solution)/shard_map/all_gather | solution.py:55
  10.1 152.0 %all-gather.13.cloned.1.call-start = ((), (), s32[]{:S(2)}) async-start(), calls=%async_computation.3 | async-start | bytes 4915200 | tf_op jit(solution)/shard_map/all_gather | solution.py:57
  10.9 188.3 %all-gather.7.cloned.1.call-start = ((), (), s32[]{:S(2)}) async-start(), calls=%async_computation | async-start | bytes 4423680 | tf_op jit(solution)/shard_map/all_gather | solution.py:30
  26.5 244.3 %all-gather.9.cloned.1.call-start = ((), (), s32[]{:S(2)}) async-start(), calls=%async_computation.1 | async-start | bytes 4423680 | tf_op jit(solution)/shard_map/all_gather | solution.py:30
  36.4 37.1 %collective-permute-start.13 = (bf16[512,896]{1,0:T(8,128)(2,1)}, bf16[512,896]{1,0:T(8,128)(2,1)}, u32[]{:S(2)}, u32[]{:S(2)}) collective-permute-start(bf16[512,896]{1,0:T(8,128)(2,1)} %get-tuple-element.161), channel_id=1, source_target_pairs={{0,8},{1,9},{2,10},{3,11},{4,12},{5,13},{6,14},{7,15}} | collective-permute-start | bytes 2752520 | tf_op jit(solution)/shard_map/ppermute | solution.py:24
  38.7 34.9 %collective-permute-start.15 = (bf16[512,896]{1,0:T(8,128)(2,1)}, bf16[512,896]{1,0:T(8,128)(2,1)}, u32[]{:S(2)}, u32[]{:S(2)}) collective-permute-start(bf16[512,896]{1,0:T(8,128)(2,1)} %get-tuple-element.160), channel_id=1, source_target_pairs={{24,16},{25,17},{26,18},{27,19},{28,20},{29,21},{30,22},{31,23}} | collective-permute-start | bytes 2752520 | tf_op jit(solution)/shard_map/ppermute | solution.py:24
  57.9 64.3 %collective-permute-start.1 = (bf16[512,896]{1,0:T(8,128)(2,1)}, bf16[512,896]{1,0:T(8,128)(2,1)S(1)}, u32[]{:S(2)}, u32[]{:S(2)}) collective-permute-start(bf16[512,896]{1,0:T(8,128)(2,1)} %get-tuple-element.173), channel_id=1, source_target_pairs={{0,8},{8,16},{1,9},{9,17},{2,10},{10,18},{3,11},{11,19},{4,12},{12... | collective-permute-start | bytes 2752520 | tf_op jit(solution)/shard_map/ppermute | solution.py:24
  62.2 60.0 %collective-permute-start.3 = (bf16[512,896]{1,0:T(8,128)(2,1)}, bf16[512,896]{1,0:T(8,128)(2,1)S(1)}, u32[]{:S(2)}, u32[]{:S(2)}) collective-permute-start(bf16[512,896]{1,0:T(8,128)(2,1)} %get-tuple-element.172), channel_id=1, source_target_pairs={{16,8},{24,16},{17,9},{25,17},{18,10},{26,18},{19,11},{27,19},{20,... | collective-permute-start | bytes 2752520 | tf_op jit(solution)/shard_map/ppermute | solution.py:24
  77.3 44.9 %collective-permute-start.14 = (bf16[512,896]{1,0:T(8,128)(2,1)}, bf16[512,896]{1,0:T(8,128)(2,1)}, u32[]{:S(2)}, u32[]{:S(2)}) collective-permute-start(bf16[512,896]{1,0:T(8,128)(2,1)} %get-tuple-element.159), channel_id=1, source_target_pairs={{0,8},{8,16},{1,9},{9,17},{2,10},{10,18},{3,11},{11,19},{4,12},{12... | collective-permute-start | bytes 2752520 | tf_op jit(solution)/shard_map/ppermute | solution.py:24
  82.7 39.6 %collective-permute-start.16 = (bf16[512,896]{1,0:T(8,128)(2,1)}, bf16[512,896]{1,0:T(8,128)(2,1)}, u32[]{:S(2)}, u32[]{:S(2)}) collective-permute-start(bf16[512,896]{1,0:T(8,128)(2,1)} %get-tuple-element.158), channel_id=1, source_target_pairs={{16,8},{24,16},{17,9},{25,17},{18,10},{26,18},{19,11},{27,19},{20,... | collective-permute-start | bytes 2752520 | tf_op jit(solution)/shard_map/ppermute | solution.py:24
  84.4 37.0 %collective-permute-start.29 = (bf16[48,5120]{1,0:T(8,128)(2,1)S(1)}, bf16[48,5120]{1,0:T(8,128)(2,1)S(1)}, u32[]{:S(2)}, u32[]{:S(2)}) collective-permute-start(bf16[48,5120]{1,0:T(8,128)(2,1)S(1)} %dynamic-slice_bitcast_fusion.4), channel_id=1, source_target_pairs={{0,16},{8,24},{16,0},{24,8},{1,17},{9,25},{17,1},{25,9},{2,18},{10... | collective-permute-start | bytes 1474568 | tf_op jit(solution)/shard_map/ppermute | solution.py:14
  146.5 27.2 %collective-permute-start.4 = (bf16[512,896]{1,0:T(8,128)(2,1)}, bf16[512,896]{1,0:T(8,128)(2,1)}, u32[]{:S(2)}, u32[]{:S(2)}) collective-permute-start(bf16[512,896]{1,0:T(8,128)(2,1)} %get-tuple-element.64), channel_id=1, source_target_pairs={{0,8},{8,16},{16,24},{1,9},{9,17},{17,25},{2,10},{10,18},{18,26},{... | collective-permute-start | bytes 2752520 | tf_op jit(solution)/shard_map/ppermute | solution.py:24
  153.5 25.5 %collective-permute-start.5 = (bf16[512,896]{1,0:T(8,128)(2,1)}, bf16[512,896]{1,0:T(8,128)(2,1)}, u32[]{:S(2)}, u32[]{:S(2)}) collective-permute-start(bf16[512,896]{1,0:T(8,128)(2,1)} %get-tuple-element.65), channel_id=1, source_target_pairs={{8,0},{16,8},{24,16},{9,1},{17,9},{25,17},{10,2},{18,10},{26,18},{... | collective-permute-start | bytes 2752520 | tf_op jit(solution)/shard_map/ppermute | solution.py:24
  154.8 35.5 %collective-permute-start.17 = (bf16[512,896]{1,0:T(8,128)(2,1)}, bf16[512,896]{1,0:T(8,128)(2,1)}, u32[]{:S(2)}, u32[]{:S(2)}) collective-permute-start(bf16[512,896]{1,0:T(8,128)(2,1)} %get-tuple-element.73), channel_id=1, source_target_pairs={{0,8},{8,16},{16,24},{1,9},{9,17},{17,25},{2,10},{10,18},{18,26},{... | collective-permute-start | bytes 2752520 | tf_op jit(solution)/shard_map/ppermute | solution.py:24
  160.4 35.0 %collective-permute-start.18 = (bf16[512,896]{1,0:T(8,128)(2,1)}, bf16[512,896]{1,0:T(8,128)(2,1)}, u32[]{:S(2)}, u32[]{:S(2)}) collective-permute-start(bf16[512,896]{1,0:T(8,128)(2,1)} %get-tuple-element.74), channel_id=1, source_target_pairs={{8,0},{16,8},{24,16},{9,1},{17,9},{25,17},{10,2},{18,10},{26,18},{... | collective-permute-start | bytes 2752520 | tf_op jit(solution)/shard_map/ppermute | solution.py:24
  209.2 28.4 %collective-permute-start.7 = (bf16[512,896]{1,0:T(8,128)(2,1)S(1)}, bf16[512,896]{1,0:T(8,128)(2,1)S(1)}, u32[]{:S(2)}, u32[]{:S(2)}) collective-permute-start(bf16[512,896]{1,0:T(8,128)(2,1)S(1)} %copy-done.32), channel_id=1, source_target_pairs={{0,8},{8,16},{16,24},{1,9},{9,17},{17,25},{2,10},{10,18},{18,26},{... | collective-permute-start | bytes 2752520 | tf_op jit(solution)/shard_map/ppermute | solution.py:24
  211.1 26.5 %collective-permute-start.8 = (bf16[512,896]{1,0:T(8,128)(2,1)S(1)}, bf16[512,896]{1,0:T(8,128)(2,1)S(1)}, u32[]{:S(2)}, u32[]{:S(2)}) collective-permute-start(bf16[512,896]{1,0:T(8,128)(2,1)S(1)} %copy-done.30), channel_id=1, source_target_pairs={{8,0},{16,8},{24,16},{9,1},{17,9},{25,17},{10,2},{18,10},{26,18},{... | collective-permute-start | bytes 2752520 | tf_op jit(solution)/shard_map/ppermute | solution.py:24
  221.1 30.4 %collective-permute-start.19 = (bf16[512,896]{1,0:T(8,128)(2,1)S(1)}, bf16[512,896]{1,0:T(8,128)(2,1)S(1)}, u32[]{:S(2)}, u32[]{:S(2)}) collective-permute-start(bf16[512,896]{1,0:T(8,128)(2,1)S(1)} %copy-done.31), channel_id=1, source_target_pairs={{0,8},{8,16},{16,24},{1,9},{9,17},{17,25},{2,10},{10,18},{18,26},{... | collective-permute-start | bytes 2752520 | tf_op jit(solution)/shard_map/ppermute | solution.py:24
  225.2 31.0 %collective-permute-start.21 = (bf16[512,896]{1,0:T(8,128)(2,1)S(1)}, bf16[512,896]{1,0:T(8,128)(2,1)S(1)}, u32[]{:S(2)}, u32[]{:S(2)}) collective-permute-start(bf16[512,896]{1,0:T(8,128)(2,1)S(1)} %copy-done.29), channel_id=1, source_target_pairs={{8,0},{16,8},{24,16},{9,1},{17,9},{25,17},{10,2},{18,10},{26,18},{... | collective-permute-start | bytes 2752520 | tf_op jit(solution)/shard_map/ppermute | solution.py:24
  235.0 102.4 %collective-permute-start.24 = (bf16[384,896]{1,0:T(8,128)(2,1)}, bf16[384,896]{1,0:T(8,128)(2,1)}, u32[]{:S(2)}, u32[]{:S(2)}) collective-permute-start(bf16[384,896]{1,0:T(8,128)(2,1)} %fusion.173), channel_id=1, source_target_pairs={{0,8},{8,0},{16,24},{24,16},{1,9},{9,1},{17,25},{25,17},{2,10},{10... | collective-permute-start | bytes 2064392 | tf_op jit(solution)/shard_map/ppermute | solution.py:14
  259.7 26.3 %collective-permute-start.20 = (bf16[512,896]{1,0:T(8,128)(2,1)}, bf16[512,896]{1,0:T(8,128)(2,1)}, u32[]{:S(2)}, u32[]{:S(2)}) collective-permute-start(bf16[512,896]{1,0:T(8,128)(2,1)} %get-tuple-element.153), channel_id=1, source_target_pairs={{0,8},{8,16},{16,24},{1,9},{9,17},{17,25},{2,10},{10,18},{18,26},{... | collective-permute-start | bytes 2752520 | tf_op jit(solution)/shard_map/ppermute | solution.py:24
  262.1 31.1 %collective-permute-start.22 = (bf16[512,896]{1,0:T(8,128)(2,1)}, bf16[512,896]{1,0:T(8,128)(2,1)}, u32[]{:S(2)}, u32[]{:S(2)}) collective-permute-start(bf16[512,896]{1,0:T(8,128)(2,1)} %get-tuple-element.152), channel_id=1, source_target_pairs={{8,0},{16,8},{24,16},{9,1},{17,9},{25,17},{10,2},{18,10},{26,18},{... | collective-permute-start | bytes 2752520 | tf_op jit(solution)/shard_map/ppermute | solution.py:24
  263.4 52.4 %collective-permute-start.10 = (bf16[512,896]{1,0:T(8,128)(2,1)}, bf16[512,896]{1,0:T(8,128)(2,1)}, u32[]{:S(2)}, u32[]{:S(2)}) collective-permute-start(bf16[512,896]{1,0:T(8,128)(2,1)} %get-tuple-element.69), channel_id=1, source_target_pairs={{8,0},{16,8},{24,16},{9,1},{17,9},{25,17},{10,2},{18,10},{26,18},{... | collective-permute-start | bytes 2752520 | tf_op jit(solution)/shard_map/ppermute | solution.py:24
  264.7 68.1 %collective-permute-start.9 = (bf16[512,896]{1,0:T(8,128)(2,1)}, bf16[512,896]{1,0:T(8,128)(2,1)}, u32[]{:S(2)}, u32[]{:S(2)}) collective-permute-start(bf16[512,896]{1,0:T(8,128)(2,1)} %get-tuple-element.68), channel_id=1, source_target_pairs={{0,8},{8,16},{16,24},{1,9},{9,17},{17,25},{2,10},{10,18},{18,26},{... | collective-permute-start | bytes 2752520 | tf_op jit(solution)/shard_map/ppermute | solution.py:24
  286.0 93.2 %collective-permute-start.31 = (bf16[384,896]{1,0:T(8,128)(2,1)S(1)}, bf16[384,896]{1,0:T(8,128)(2,1)S(1)}, u32[]{:S(2)}, u32[]{:S(2)}) collective-permute-start(bf16[384,896]{1,0:T(8,128)(2,1)S(1)} %fusion.167), channel_id=1, source_target_pairs={{0,16},{8,24},{16,0},{24,8},{1,17},{9,25},{17,1},{25,9},{2,18},{10... | collective-permute-start | bytes 2064392 | tf_op jit(solution)/shard_map/ppermute | solution.py:14
  293.2 86.2 %collective-permute-start.30 = (bf16[384,896]{1,0:T(8,128)(2,1)S(1)}, bf16[384,896]{1,0:T(8,128)(2,1)S(1)}, u32[]{:S(2)}, u32[]{:S(2)}) collective-permute-start(bf16[384,896]{1,0:T(8,128)(2,1)S(1)} %fusion.179), channel_id=1, source_target_pairs={{0,16},{8,24},{16,0},{24,8},{1,17},{9,25},{17,1},{25,9},{2,18},{10... | collective-permute-start | bytes 2064392 | tf_op jit(solution)/shard_map/ppermute | solution.py:14
  315.8 42.2 %collective-permute-start.23 = (bf16[384,896]{1,0:T(8,128)(2,1)S(1)}, bf16[384,896]{1,0:T(8,128)(2,1)S(1)}, u32[]{:S(2)}, u32[]{:S(2)}) collective-permute-start(bf16[384,896]{1,0:T(8,128)(2,1)S(1)} %copy-done.38), channel_id=1, source_target_pairs={{0,8},{8,0},{16,24},{24,16},{1,9},{9,1},{17,25},{25,17},{2,10},{10... | collective-permute-start | bytes 2064392 | tf_op jit(solution)/shard_map/ppermute | solution.py:14
  335.2 34.3 %collective-permute-start.11 = (bf16[512,896]{1,0:T(8,128)(2,1)S(1)}, bf16[512,896]{1,0:T(8,128)(2,1)S(1)}, u32[]{:S(2)}, u32[]{:S(2)}) collective-permute-start(bf16[512,896]{1,0:T(8,128)(2,1)S(1)} %get-tuple-element.70), channel_id=1, source_target_pairs={{0,8},{8,16},{16,24},{1,9},{9,17},{17,25},{2,10},{10,18},{18,26},{... | collective-permute-start | bytes 2752520 | tf_op jit(solution)/shard_map/ppermute | solution.py:24
  337.4 38.3 %collective-permute-start.12 = (bf16[512,896]{1,0:T(8,128)(2,1)S(1)}, bf16[512,896]{1,0:T(8,128)(2,1)S(1)}, u32[]{:S(2)}, u32[]{:S(2)}) collective-permute-start(bf16[512,896]{1,0:T(8,128)(2,1)S(1)} %get-tuple-element.71), channel_id=1, source_target_pairs={{8,0},{16,8},{24,16},{9,1},{17,9},{25,17},{10,2},{18,10},{26,18},{... | collective-permute-start | bytes 2752520 | tf_op jit(solution)/shard_map/ppermute | solution.py:24
  358.0 27.1 %collective-permute-start.27 = (bf16[512,896]{1,0:T(8,128)(2,1)S(1)}, bf16[512,896]{1,0:T(8,128)(2,1)S(1)}, u32[]{:S(2)}, u32[]{:S(2)}) collective-permute-start(bf16[512,896]{1,0:T(8,128)(2,1)S(1)} %get-tuple-element.87), channel_id=1, source_target_pairs={{0,8},{8,16},{16,24},{1,9},{9,17},{17,25},{2,10},{10,18},{18,26},{... | collective-permute-start | bytes 2752520 | tf_op jit(solution)/shard_map/ppermute | solution.py:24
  395.5 44.6 %collective-permute-start.42 = (bf16[512,896]{1,0:T(8,128)(2,1)}, bf16[512,896]{1,0:T(8,128)(2,1)}, u32[]{:S(2)}, u32[]{:S(2)}) collective-permute-start(bf16[512,896]{1,0:T(8,128)(2,1)} %get-tuple-element.108), channel_id=1, source_target_pairs={{0,8},{8,16},{16,24},{1,9},{9,17},{17,25},{2,10},{10,18},{18,26},{... | collective-permute-start | bytes 2752520 | tf_op jit(solution)/shard_map/ppermute | solution.py:24
  402.6 37.5 %collective-permute-start.43 = (bf16[512,896]{1,0:T(8,128)(2,1)}, bf16[512,896]{1,0:T(8,128)(2,1)}, u32[]{:S(2)}, u32[]{:S(2)}) collective-permute-start(bf16[512,896]{1,0:T(8,128)(2,1)} %get-tuple-element.109), channel_id=1, source_target_pairs={{8,0},{16,8},{24,16},{9,1},{17,9},{25,17},{10,2},{18,10},{26,18},{... | collective-permute-start | bytes 2752520 | tf_op jit(solution)/shard_map/ppermute | solution.py:24
  403.9 45.7 %collective-permute-start.25 = (bf16[512,896]{1,0:T(8,128)(2,1)}, bf16[512,896]{1,0:T(8,128)(2,1)}, u32[]{:S(2)}, u32[]{:S(2)}) collective-permute-start(bf16[512,896]{1,0:T(8,128)(2,1)} %get-tuple-element.85), channel_id=1, source_target_pairs={{0,8},{8,16},{16,24},{1,9},{9,17},{17,25},{2,10},{10,18},{18,26},{... | collective-permute-start | bytes 2752520 | tf_op jit(solution)/shard_map/ppermute | solution.py:24
  410.6 39.1 %collective-permute-start.26 = (bf16[512,896]{1,0:T(8,128)(2,1)}, bf16[512,896]{1,0:T(8,128)(2,1)}, u32[]{:S(2)}, u32[]{:S(2)}) collective-permute-start(bf16[512,896]{1,0:T(8,128)(2,1)} %get-tuple-element.86), channel_id=1, source_target_pairs={{8,0},{16,8},{24,16},{9,1},{17,9},{25,17},{10,2},{18,10},{26,18},{... | collective-permute-start | bytes 2752520 | tf_op jit(solution)/shard_map/ppermute | solution.py:24
  443.3 35.4 %collective-permute-start.44 = (bf16[512,896]{1,0:T(8,128)(2,1)}, bf16[512,896]{1,0:T(8,128)(2,1)S(1)}, u32[]{:S(2)}, u32[]{:S(2)}) collective-permute-start(bf16[512,896]{1,0:T(8,128)(2,1)} %get-tuple-element.111), channel_id=1, source_target_pairs={{0,8},{8,16},{16,24},{1,9},{9,17},{17,25},{2,10},{10,18},{18,26},{... | collective-permute-start | bytes 2752520 | tf_op jit(solution)/shard_map/ppermute | solution.py:24
  448.3 30.5 %collective-permute-start.45 = (bf16[512,896]{1,0:T(8,128)(2,1)}, bf16[512,896]{1,0:T(8,128)(2,1)S(1)}, u32[]{:S(2)}, u32[]{:S(2)}) collective-permute-start(bf16[512,896]{1,0:T(8,128)(2,1)} %get-tuple-element.112), channel_id=1, source_target_pairs={{8,0},{16,8},{24,16},{9,1},{17,9},{25,17},{10,2},{18,10},{26,18},{... | collective-permute-start | bytes 2752520 | tf_op jit(solution)/shard_map/ppermute | solution.py:24
  453.0 34.0 %collective-permute-start.32 = (bf16[512,896]{1,0:T(8,128)(2,1)}, bf16[512,896]{1,0:T(8,128)(2,1)S(1)}, u32[]{:S(2)}, u32[]{:S(2)}) collective-permute-start(bf16[512,896]{1,0:T(8,128)(2,1)} %get-tuple-element.93), channel_id=1, source_target_pairs={{0,8},{8,16},{16,24},{1,9},{9,17},{17,25},{2,10},{10,18},{18,26},{... | collective-permute-start | bytes 2752520 | tf_op jit(solution)/shard_map/ppermute | solution.py:24
  457.9 29.1 %collective-permute-start.33 = (bf16[512,896]{1,0:T(8,128)(2,1)}, bf16[512,896]{1,0:T(8,128)(2,1)}, u32[]{:S(2)}, u32[]{:S(2)}) collective-permute-start(bf16[512,896]{1,0:T(8,128)(2,1)} %get-tuple-element.94), channel_id=1, source_target_pairs={{8,0},{16,8},{24,16},{9,1},{17,9},{25,17},{10,2},{18,10},{26,18},{... | collective-permute-start | bytes 2752520 | tf_op jit(solution)/shard_map/ppermute | solution.py:24
  480.5 35.0 %collective-permute-start.46 = (bf16[512,896]{1,0:T(8,128)(2,1)}, bf16[512,896]{1,0:T(8,128)(2,1)S(1)}, u32[]{:S(2)}, u32[]{:S(2)}) collective-permute-start(bf16[512,896]{1,0:T(8,128)(2,1)} %get-tuple-element.114), channel_id=1, source_target_pairs={{0,8},{8,16},{16,24},{1,9},{9,17},{17,25},{2,10},{10,18},{18,26},{... | collective-permute-start | bytes 2752520 | tf_op jit(solution)/shard_map/ppermute | solution.py:24
  485.7 29.8 %collective-permute-start.47 = (bf16[512,896]{1,0:T(8,128)(2,1)}, bf16[512,896]{1,0:T(8,128)(2,1)S(1)}, u32[]{:S(2)}, u32[]{:S(2)}) collective-permute-start(bf16[512,896]{1,0:T(8,128)(2,1)} %get-tuple-element.115), channel_id=1, source_target_pairs={{8,0},{16,8},{24,16},{9,1},{17,9},{25,17},{10,2},{18,10},{26,18},{... | collective-permute-start | bytes 2752520 | tf_op jit(solution)/shard_map/ppermute | solution.py:24
  489.9 33.6 %collective-permute-start.34 = (bf16[512,896]{1,0:T(8,128)(2,1)}, bf16[512,896]{1,0:T(8,128)(2,1)}, u32[]{:S(2)}, u32[]{:S(2)}) collective-permute-start(bf16[512,896]{1,0:T(8,128)(2,1)} %get-tuple-element.96), channel_id=1, source_target_pairs={{0,8},{8,16},{16,24},{1,9},{9,17},{17,25},{2,10},{10,18},{18,26},{... | collective-permute-start | bytes 2752520 | tf_op jit(solution)/shard_map/ppermute | solution.py:24
  495.4 28.8 %collective-permute-start.35 = (bf16[512,896]{1,0:T(8,128)(2,1)}, bf16[512,896]{1,0:T(8,128)(2,1)}, u32[]{:S(2)}, u32[]{:S(2)}) collective-permute-start(bf16[512,896]{1,0:T(8,128)(2,1)} %get-tuple-element.97), channel_id=1, source_target_pairs={{8,0},{16,8},{24,16},{9,1},{17,9},{25,17},{10,2},{18,10},{26,18},{... | collective-permute-start | bytes 2752520 | tf_op jit(solution)/shard_map/ppermute | solution.py:24
  531.3 36.0 %collective-permute-start.37 = (bf16[512,896]{1,0:T(8,128)(2,1)}, bf16[512,896]{1,0:T(8,128)(2,1)S(1)}, u32[]{:S(2)}, u32[]{:S(2)}) collective-permute-start(bf16[512,896]{1,0:T(8,128)(2,1)} %get-tuple-element.100), channel_id=1, source_target_pairs={{8,0},{16,8},{24,16},{9,1},{17,9},{25,17},{10,2},{18,10},{26,18},{... | collective-permute-start | bytes 2752520 | tf_op jit(solution)/shard_map/ppermute | solution.py:24
  549.4 30.6 %collective-permute-start.50 = (bf16[512,896]{1,0:T(8,128)(2,1)}, bf16[512,896]{1,0:T(8,128)(2,1)}, u32[]{:S(2)}, u32[]{:S(2)}) collective-permute-start(bf16[512,896]{1,0:T(8,128)(2,1)} %get-tuple-element.120), channel_id=1, source_target_pairs={{8,16},{16,24},{9,17},{17,25},{10,18},{18,26},{11,19},{19,27},{12,... | collective-permute-start | bytes 2752520 | tf_op jit(solution)/shard_map/ppermute | solution.py:24
  551.0 36.1 %collective-permute-start.51 = (bf16[512,896]{1,0:T(8,128)(2,1)}, bf16[512,896]{1,0:T(8,128)(2,1)}, u32[]{:S(2)}, u32[]{:S(2)}) collective-permute-start(bf16[512,896]{1,0:T(8,128)(2,1)} %get-tuple-element.121), channel_id=1, source_target_pairs={{8,0},{16,8},{9,1},{17,9},{10,2},{18,10},{11,3},{19,11},{12,4},{20... | collective-permute-start | bytes 2752520 | tf_op jit(solution)/shard_map/ppermute | solution.py:24
  570.7 36.0 %collective-permute-start.39 = (bf16[512,896]{1,0:T(8,128)(2,1)}, bf16[512,896]{1,0:T(8,128)(2,1)}, u32[]{:S(2)}, u32[]{:S(2)}) collective-permute-start(bf16[512,896]{1,0:T(8,128)(2,1)} %get-tuple-element.103), channel_id=1, source_target_pairs={{8,0},{16,8},{9,1},{17,9},{10,2},{18,10},{11,3},{19,11},{12,4},{20... | collective-permute-start | bytes 2752520 | tf_op jit(solution)/shard_map/ppermute | solution.py:24
  588.9 33.1 %collective-permute-start.52 = (bf16[512,896]{1,0:T(8,128)(2,1)S(1)}, bf16[512,896]{1,0:T(8,128)(2,1)}, u32[]{:S(2)}, u32[]{:S(2)}) collective-permute-start(bf16[512,896]{1,0:T(8,128)(2,1)S(1)} %get-tuple-element.124), channel_id=1, source_target_pairs={{16,24},{17,25},{18,26},{19,27},{20,28},{21,29},{22,30},{23,31}} | collective-permute-start | bytes 2752520 | tf_op jit(solution)/shard_map/ppermute | solution.py:24
  590.5 34.9 %collective-permute-start.53 = (bf16[512,896]{1,0:T(8,128)(2,1)S(1)}, bf16[512,896]{1,0:T(8,128)(2,1)}, u32[]{:S(2)}, u32[]{:S(2)}) collective-permute-start(bf16[512,896]{1,0:T(8,128)(2,1)S(1)} %get-tuple-element.125), channel_id=1, source_target_pairs={{8,0},{9,1},{10,2},{11,3},{12,4},{13,5},{14,6},{15,7}} | collective-permute-start | bytes 2752520 | tf_op jit(solution)/shard_map/ppermute | solution.py:24
  (64 other events, 1061.5 us)
Sparse Core Ops, SparseCore 0:
  10.2 35.6 all-gather.10
  48.1 32.9 all-gather.12
  83.0 35.6 all-gather.6
  122.3 37.2 all-gather.8
